TPU v7x, 32 devices: a whole 2x2x4 slice. The times are simulated.
32 devices in a mesh: groups: 2 (over x), dp: 16 (over z, y, core).
Axes of the slice: x: 2, y: 2, z: 4, core: 2. Of those that a mesh axis runs over, the one named last changes fastest.
Arguments:
- tokens: bfloat16 [4096, 8192], P(('groups', 'dp')), parts along dimension 0, may hold values from -6 to 6
- out_grad: bfloat16 [4096, 512], P(('groups', 'dp')), parts along dimension 0, may hold values from -6 to 6
- base_weight: bfloat16 [8192, 512], P('dp'), may hold values from -0.0625 to 0.0625
- adapter_down: bfloat16 [16, 64, 8192], P(None, None, 'dp'), may hold values from -0.0625 to 0.0625
- adapter_up: bfloat16 [16, 32768], P(None, 'dp'), may hold values from -0.75 to 0.75
- rank_tiles: int32 [16], replicated, may hold values from 1 to 4, as said below
- tile_adapter: int32 [32, 1], P('groups'), parts along dimension 0, may hold values from 0 to 15
Outputs:
- result: bfloat16 [4096, 512], P(('groups', 'dp')), parts along dimension 0
- grad_in: bfloat16 [4096, 8192], P(('groups', 'dp')), parts along dimension 0
- down_grad: bfloat16 [32, 64, 8192], P('groups', None, 'dp'), parts along dimension 0
- up_grad: bfloat16 [32, 32768], P('groups', 'dp'), parts along dimension 0
There are 2 independent parts, one for each index of `groups`. A program takes and returns all parts, laid end to end along the dimension named above; an argument that names none is the same for every part. Nothing has to cross between parts.
Inputs may be any that keep to these rules, and one draw needn't show every extreme that they name: `rank_tiles`: ranks of 1 and of 4 tiles occur in every draw. `tile_adapter`: every adapter is used by at least one tile.
All inputs are finite; a program needn't handle non-finite values.
Results may differ from a plain program's by a relative error of at most 0.005.
Values may be sent and summed in bfloat16 or wider, within the bound.
No kernel may reach another device: no remote copies, remote signals or barrier semaphores. Data moves between devices by JAX's collectives and lax.ppermute only.
A program may use at most 64 MiB of HBM per device.

v0:
```python
import jax
import jax.numpy as jnp
from jax import lax
from jax.sharding import PartitionSpec as P

RANK_TILE = 16
TILE = 128


def rank_factor(adapter_ids, rank_tiles, rank_width):
    adapter_count = rank_tiles.shape[0]
    matches = adapter_ids[:, None] == jnp.arange(adapter_count, dtype=jnp.int32)[None, :]
    tile_ranks = jnp.sum(jnp.where(matches, rank_tiles[None, :], 0), axis=1)
    columns = jnp.arange(rank_width, dtype=jnp.int32)
    kept_mask = (columns[None, :] < tile_ranks[:, None] * RANK_TILE).astype(jnp.float32)
    return kept_mask * (2.0 / tile_ranks.astype(jnp.float32))[:, None]


def per_adapter(all_ids, terms, adapter_count):
    onehot = (all_ids[:, None] == jnp.arange(adapter_count, dtype=jnp.int32)[None, :]).astype(
        jnp.float32
    )
    flat_terms = terms.reshape(terms.shape[0], -1)
    summed = jnp.dot(
        onehot.T, flat_terms, precision=lax.Precision.HIGHEST, preferred_element_type=jnp.float32
    )
    return summed.reshape((adapter_count,) + terms.shape[1:])


def body(tokens, out_grad, base_weight, adapter_down, adapter_up, rank_tiles, tile_adapter):
    tok_rows = tokens.shape[0]
    model_width = tokens.shape[1]
    out_width = out_grad.shape[1]
    adapter_count = adapter_down.shape[0]
    rank_width = adapter_down.shape[1]
    tiles_dev = tok_rows // TILE
    all_ids = tile_adapter[:, 0]
    position = lax.axis_index("dp")
    my_ids = lax.dynamic_slice_in_dim(all_ids, position * tiles_dev, tiles_dev)
    factor = rank_factor(my_ids, rank_tiles, rank_width)
    weight_rows = lax.all_gather(base_weight, "dp", axis=0, tiled=True)
    forward = jnp.dot(tokens, weight_rows, preferred_element_type=jnp.float32)
    grad_cols = jnp.dot(out_grad, weight_rows.T, preferred_element_type=jnp.float32)
    grad_tiles = out_grad.reshape(tiles_dev, TILE, out_width)
    sliced = lax.all_to_all(tokens, "dp", split_axis=1, concat_axis=0, tiled=True)
    slice_tiles = sliced.reshape(all_ids.shape[0], TILE, sliced.shape[1])
    down_all = adapter_down[all_ids]
    lowrank = lax.psum_scatter(
        jnp.einsum("tsd,trd->tsr", slice_tiles, down_all, preferred_element_type=jnp.float32),
        "dp",
        scatter_dimension=0,
        tiled=True,
    )
    up_flat = lax.all_to_all(adapter_up[all_ids], "dp", split_axis=0, concat_axis=1, tiled=True)
    up_tiles = up_flat.reshape(tiles_dev, out_width, rank_width)
    hidden = (lowrank * factor[:, None, :]).astype(jnp.bfloat16)
    out_low = jnp.einsum("tsr,tor->tso", hidden, up_tiles, preferred_element_type=jnp.float32)
    backward_rank = jnp.einsum(
        "tso,tor->tsr", grad_tiles, up_tiles, preferred_element_type=jnp.float32
    )
    backward_rank = (backward_rank * factor[:, None, :]).astype(jnp.bfloat16)
    up_terms = jnp.einsum("tso,tsr->tor", grad_tiles, hidden, preferred_element_type=jnp.float32)
    rank_all = lax.all_gather(backward_rank, "dp", axis=0, tiled=True)
    slice_grads = jnp.einsum(
        "tsr,trd->tsd", rank_all, down_all, preferred_element_type=jnp.float32
    ).astype(jnp.bfloat16)
    in_low = lax.all_to_all(slice_grads, "dp", split_axis=0, concat_axis=2, tiled=True)
    down_terms = jnp.einsum(
        "tsr,tsd->trd", rank_all, slice_tiles, preferred_element_type=jnp.float32
    )
    down_grad = per_adapter(all_ids, down_terms, adapter_count)
    up_back = lax.all_to_all(
        up_terms.reshape(tiles_dev, -1), "dp", split_axis=1, concat_axis=0, tiled=True
    )
    up_grad = per_adapter(all_ids, up_back, adapter_count)
    result = (forward + out_low.reshape(tok_rows, out_width)).astype(jnp.bfloat16)
    grad_in = (grad_cols + in_low.reshape(tok_rows, model_width).astype(jnp.float32)).astype(
        jnp.bfloat16
    )
    return (result, grad_in, down_grad.astype(jnp.bfloat16), up_grad.astype(jnp.bfloat16))


def solution(mesh):
    return jax.shard_map(
        body,
        mesh=mesh,
        in_specs=(
            P(("groups", "dp"), None),
            P(("groups", "dp"), None),
            P("dp", None),
            P(None, None, "dp"),
            P(None, "dp"),
            P(),
            P("groups", None),
        ),
        out_specs=(
            P(("groups", "dp"), None),
            P(("groups", "dp"), None),
            P("groups", None, "dp"),
            P("groups", "dp"),
        ),
        check_vma=False,
    )
```

profile of v0, /device:TPU:0, one launch (start us, length us, event | category | flops | bytes accessed | tf_op | source)
XLA Modules:
  0.0 244.3 jit_solution(8165552851586583453)
XLA Ops:
  7.2 0.0 copy-start
  7.2 3.3 %copy.23 = bf16[128,8192]{0,1:T(8,128)(2,1)S(1)} copy(bf16[128,8192]{1,0:T(8,128)(2,1)} %param.7) | data formatting | bytes 4194304 | tf_op args[0]
  10.5 2.6 %copy.24 = bf16[128,16,512]{2,0,1:T(8,128)(2,1)} copy(bf16[128,16,512]{0,2,1:T(8,128)(2,1)S(1)} %bitcast.80) | data formatting | bytes 4194304 | tf_op jit(solution)/shard_map/all_to_all | solution.py:45
  13.1 0.0 copy-start.9
  13.1 7.5 %all-to-all-start = ((bf16[128,16,512]{2,0,1:T(8,128)(2,1)}), bf16[128,16,512]{2,0,1:T(8,128)(2,1)S(1)}, u32[]{:S(2)}, u32[]{:S(2)}) async-start(bf16[128,16,512]{2,0,1:T(8,128)(2,1)} %copy.24), calls=%async_computation | async-start | bytes 4194304 | tf_op jit(solution)/shard_map/all_to_all | solution.py:45
  20.6 0.0 reduce-scatter.2.cloned.1.call-start
  20.7 0.0 copy-done.9
  20.7 0.0 copy-done
  20.7 1.6 gather_fusion
  22.3 0.0 copy-start.4
  22.3 0.0 copy-start.10
  22.3 39.4 %all-to-all-done = bf16[128,16,512]{2,0,1:T(8,128)(2,1)S(1)} async-done(((bf16[128,16,512]{2,0,1:T(8,128)(2,1)}), bf16[128,16,512]{2,0,1:T(8,128)(2,1)S(1)}, u32[]{:S(2)}, u32[]{:S(2)}) %all-to-all-start) | async-done | bytes 2097184 | tf_op jit(solution)/shard_map/all_to_all | solution.py:45
  61.7 2.9 %fusion.11 = f32[16,128,64]{1,2,0:T(8,128)} fusion(bf16[16,64,512]{2,1,0:T(8,128)(2,1)} %gather_fusion, bf16[128,16,512]{2,0,1:T(8,128)(2,1)S(1)} %all-to-all-done), kind=kOutput, calls=%fused_computation.15 | convolution fusion | flops 134217728 | bytes 3670016 | tf_op jit(solution)/shard_map/tsd,trd->tsr/dot_general | solution.py:49
  64.6 0.0 copy-start.5
  64.6 0.0 reduce-scatter.2.cloned.1.call-update
  64.6 0.0 all-gather.3.cloned.1.call-start
  64.7 0.7 all-gather.3.cloned.1.call-update
  65.4 0.0 copy-done.4
  65.4 0.6 gather_fusion.1
  66.0 0.5 broadcast.52
  66.5 0.7 reduce.3
  67.2 0.7 reshape.118
  67.8 11.2 %all-to-all-start.1 = ((bf16[16,2,1024]{2,1,0:T(2,128)(2,1)}), bf16[16,2,1024]{2,1,0:T(2,128)(2,1)S(1)}, u32[]{:S(2)}, u32[]{:S(2)}) async-start(bf16[16,2,1024]{2,1,0:T(2,128)(2,1)} %reshape.118), calls=%async_computation.2 | async-start | bytes 131072 | tf_op jit(solution)/shard_map/all_to_all | solution.py:54
  79.0 0.6 constant_dynamic-slice_fusion
  79.6 0.0 copy-done.10
  79.6 1.3 fusion.28
  82.3 3.7 %all-to-all-done.1 = bf16[16,2,1024]{2,1,0:T(2,128)(2,1)S(1)} async-done(((bf16[16,2,1024]{2,1,0:T(2,128)(2,1)}), bf16[16,2,1024]{2,1,0:T(2,128)(2,1)S(1)}, u32[]{:S(2)}, u32[]{:S(2)}) %all-to-all-start.1) | async-done | bytes 65568 | tf_op jit(solution)/shard_map/all_to_all | solution.py:54
  85.9 0.1 reshape.119
  86.0 0.4 reduce.2
  86.4 0.2 reshape.95
  86.5 0.0 copy-start.6
  86.5 0.6 copy-done.6
  87.2 0.0 copy-done.5
  87.2 0.2 fusion.16
  87.4 19.2 %all-gather = bf16[2048,64]{0,1:T(8,128)(2,1)S(1)} all-gather(bf16[128,64]{0,1:T(8,128)(2,1)S(1)} %fusion.16), channel_id=2, replica_groups=mesh['groups'=2,'dp'=16] {'dp'}, dimensions={0}, use_global_device_ids=true | all-gather | bytes 278528 | tf_op jit(solution)/shard_map/all_gather | solution.py:63
  106.6 3.3 %convolution_convert_fusion.1 = bf16[16,128,512]{2,1,0:T(8,128)(2,1)} fusion(bf16[16,64,512]{2,1,0:T(8,128)(2,1)} %gather_fusion, bf16[2048,64]{0,1:T(8,128)(2,1)S(1)} %all-gather), kind=kOutput, calls=%fused_computation.13 | convolution fusion | flops 135266304 | bytes 3407872 | tf_op jit(solution)/shard_map/tsr,trd->tsd/dot_general | solution.py:64
  109.9 4.4 %all-to-all-start.2 = ((bf16[16,128,512]{2,1,0:T(8,128)(2,1)}), bf16[16,128,512]{2,1,0:T(8,128)(2,1)}, u32[]{:S(2)}, u32[]{:S(2)}) async-start(bf16[16,128,512]{2,1,0:T(8,128)(2,1)} %convolution_convert_fusion.1), calls=%async_computation.3 | async-start | bytes 4194304 | tf_op jit(solution)/shard_map/all_to_all | solution.py:67
  114.3 0.4 fusion.4
  114.7 2.3 fusion.8
  117.1 1.5 copy.32
  118.6 15.0 %reduce-scatter.2.cloned.1.call-done = f32[1,128,64]{1,2,0:T(8,128)} async-done(((f32[16,128,64]{1,2,0:T(8,128)}), f32[1,128,64]{1,2,0:T(8,128)}) %reduce-scatter.2.cloned.1.call-update) | async-done | bytes 32784 | tf_op jit(solution)/shard_map/reduce_scatter | solution.py:48
  133.6 0.9 convolution_bitcast_fusion
  134.6 0.1 copy.30
  134.7 0.8 all_to_all.50
  135.6 30.1 %all-to-all-done.2 = bf16[16,128,512]{2,1,0:T(8,128)(2,1)} async-done(((bf16[16,128,512]{2,1,0:T(8,128)(2,1)}), bf16[16,128,512]{2,1,0:T(8,128)(2,1)}, u32[]{:S(2)}, u32[]{:S(2)}) %all-to-all-start.2) | async-done | bytes 2097184 | tf_op jit(solution)/shard_map/all_to_all | solution.py:67
  165.7 18.7 %all-to-all-start.3 = ((f32[1,16,2048]{2,0,1:T(1,128)}), f32[1,16,2048]{2,0,1:T(1,128)S(1)}, u32[]{:S(2)}, u32[]{:S(2)}) async-start(f32[1,16,2048]{2,0,1:T(1,128)} %all_to_all.50), calls=%async_computation.4 | async-start | bytes 262144 | tf_op jit(solution)/shard_map/all_to_all | solution.py:72
  184.4 2.1 fusion.32
  186.5 0.0 copy-start.3
  186.5 2.6 %copy.36 = f32[16,8,16,512]{3,1,2,0:T(8,128)} copy(f32[16,8,16,512]{3,1,0,2:T(8,128)S(1)} %fusion.32) | data formatting | bytes 8388608
  189.2 5.6 %all-to-all-done.3 = f32[1,16,2048]{2,0,1:T(1,128)S(1)} async-done(((f32[1,16,2048]{2,0,1:T(1,128)}), f32[1,16,2048]{2,0,1:T(1,128)S(1)}, u32[]{:S(2)}, u32[]{:S(2)}) %all-to-all-start.3) | async-done | bytes 131104 | tf_op jit(solution)/shard_map/all_to_all | solution.py:72
  194.7 0.9 convolution_convert_fusion
  195.6 29.8 %all-gather.3.cloned.1.call-done = bf16[8192,512]{1,0:T(8,128)(2,1)} async-done(((bf16[512,512]{1,0:T(8,128)(2,1)}), bf16[8192,512]{1,0:T(8,128)(2,1)}) %all-gather.3.cloned.1.call-update) | async-done | bytes 8388624 | tf_op jit(solution)/shard_map/all_gather | solution.py:41
  225.4 0.0 copy-done.3
  225.4 0.0 copy-start.1
  225.4 0.0 copy-start.2
  225.4 4.8 %fusion.33 = f32[128,512]{1,0:T(8,128)S(1)} fusion(bf16[128,8192]{1,0:T(8,128)(2,1)S(1)} %copy-done.3, bf16[8192,512]{1,0:T(8,128)(2,1)} %all-gather.3.cloned.1.call-done), kind=kOutput, calls=%fused_computation.43 | convolution fusion | flops 1073741824 | bytes 10747904 | tf_op jit(solution)/shard_map/dot_general | solution.py:42
  230.2 1.0 copy-done.1
  231.2 1.2 copy-done.2
  232.4 0.0 copy-start.7
  232.4 0.0 copy-start.8
  232.4 4.2 %fusion = bf16[128,8192]{1,0:T(8,128)(2,1)} fusion(f32[128,8192]{1,0:T(8,128)S(1)} %bitcast.78, bf16[128,512]{1,0:T(8,128)(2,1)S(1)} %copy-done.5, bf16[8192,512]{1,0:T(8,128)(2,1)S(1)} %copy-done.1), kind=kOutput, calls=%fused_computation.3 | convolution fusion | flops 1075838976 | bytes 14811136 | tf_op jit(solution)/shard_map/dot_general | solution.py:43
  236.6 0.0 copy-done.7
  236.6 0.0 copy-done.8
  236.6 0.9 fusion.14
  (3 shorter events, 0.0 us)
Async XLA Ops:
  7.2 13.5 %copy-start = (bf16[16,64,512]{2,1,0:T(8,128)(2,1)S(1)}, bf16[16,64,512]{2,1,0:T(8,128)(2,1)}, u32[]{:S(2)}) copy-start(bf16[16,64,512]{2,1,0:T(8,128)(2,1)} %param.10) | copy-start | bytes 3145732
  13.1 7.6 %copy-start.9 = (s32[16,1]{0,1:T(1,128)S(1)}, s32[16,1]{0,1:T(1,128)}, u32[]{:S(2)}) copy-start(s32[16,1]{0,1:T(1,128)} %param.13) | copy-start | bytes 196
  13.1 48.6 %all-to-all-start = ((bf16[128,16,512]{2,0,1:T(8,128)(2,1)}), bf16[128,16,512]{2,0,1:T(8,128)(2,1)S(1)}, u32[]{:S(2)}, u32[]{:S(2)}) async-start(bf16[128,16,512]{2,0,1:T(8,128)(2,1)} %copy.24), calls=%async_computation | async-start | bytes 4194304 | tf_op jit(solution)/shard_map/all_to_all | solution.py:45
  20.6 113.0 %reduce-scatter.2.cloned.1.call-start = ((), (), s32[]{:S(2)}) async-start(), calls=%async_computation.6 | async-start | bytes 557056 | tf_op jit(solution)/shard_map/reduce_scatter | solution.py:48
  22.3 43.1 %copy-start.4 = (bf16[16,2048]{1,0:T(8,128)(2,1)S(1)}, bf16[16,2048]{1,0:T(8,128)(2,1)}, u32[]{:S(2)}) copy-start(bf16[16,2048]{1,0:T(8,128)(2,1)} %param.11) | copy-start | bytes 196612
  22.3 57.3 %copy-start.10 = (s32[16]{0:T(128)S(1)}, s32[16]{0:T(128)}, u32[]{:S(2)}) copy-start(s32[16]{0:T(128)} %param.12) | copy-start | bytes 196
  64.6 22.6 %copy-start.5 = (bf16[128,512]{1,0:T(8,128)(2,1)S(1)}, bf16[128,512]{1,0:T(8,128)(2,1)}, u32[]{:S(2)}) copy-start(bf16[128,512]{1,0:T(8,128)(2,1)} %param.8) | copy-start | bytes 393220
  64.6 160.8 %all-gather.3.cloned.1.call-start = ((), (), s32[]{:S(2)}) async-start(), calls=%async_computation.5 | async-start | bytes 8912896 | tf_op jit(solution)/shard_map/all_gather | solution.py:41
  67.8 18.1 %all-to-all-start.1 = ((bf16[16,2,1024]{2,1,0:T(2,128)(2,1)}), bf16[16,2,1024]{2,1,0:T(2,128)(2,1)S(1)}, u32[]{:S(2)}, u32[]{:S(2)}) async-start(bf16[16,2,1024]{2,1,0:T(2,128)(2,1)} %reshape.118), calls=%async_computation.2 | async-start | bytes 131072 | tf_op jit(solution)/shard_map/all_to_all | solution.py:54
  86.5 0.7 copy-start.6
  109.9 55.8 %all-to-all-start.2 = ((bf16[16,128,512]{2,1,0:T(8,128)(2,1)}), bf16[16,128,512]{2,1,0:T(8,128)(2,1)}, u32[]{:S(2)}, u32[]{:S(2)}) async-start(bf16[16,128,512]{2,1,0:T(8,128)(2,1)} %convolution_convert_fusion.1), calls=%async_computation.3 | async-start | bytes 4194304 | tf_op jit(solution)/shard_map/all_to_all | solution.py:67
  165.7 29.1 %all-to-all-start.3 = ((f32[1,16,2048]{2,0,1:T(1,128)}), f32[1,16,2048]{2,0,1:T(1,128)S(1)}, u32[]{:S(2)}, u32[]{:S(2)}) async-start(f32[1,16,2048]{2,0,1:T(1,128)} %all_to_all.50), calls=%async_computation.4 | async-start | bytes 262144 | tf_op jit(solution)/shard_map/all_to_all | solution.py:72
  186.5 38.9 %copy-start.3 = (bf16[128,8192]{1,0:T(8,128)(2,1)S(1)}, bf16[128,8192]{1,0:T(8,128)(2,1)}, u32[]{:S(2)}) copy-start(bf16[128,8192]{1,0:T(8,128)(2,1)} %param.7) | copy-start | bytes 6291460
  225.4 5.8 %copy-start.1 = (bf16[8192,512]{1,0:T(8,128)(2,1)S(1)}, bf16[8192,512]{1,0:T(8,128)(2,1)}, u32[]{:S(2)}) copy-start(bf16[8192,512]{1,0:T(8,128)(2,1)} %all-gather.3.cloned.1.call-done) | copy-start | bytes 25165828
  225.4 7.0 %copy-start.2 = (f32[16,8,16,512]{3,1,2,0:T(8,128)S(1)}, f32[16,8,16,512]{3,1,2,0:T(8,128)}, u32[]{:S(2)}) copy-start(f32[16,8,16,512]{3,1,2,0:T(8,128)} %copy.36) | copy-start | bytes 12582916
  232.4 4.2 %copy-start.7 = (bf16[512,64]{1,0:T(8,128)(2,1)S(1)}, bf16[512,64]{1,0:T(8,128)(2,1)}, u32[]{:S(2)}) copy-start(bf16[512,64]{1,0:T(8,128)(2,1)} %copy-done.6) | copy-start | bytes 196612
  232.4 4.2 %copy-start.8 = (f32[1,128,64]{1,2,0:T(8,128)S(1)}, f32[1,128,64]{1,2,0:T(8,128)}, u32[]{:S(2)}) copy-start(f32[1,128,64]{1,2,0:T(8,128)} %reduce-scatter.2.cloned.1.call-done) | copy-start | bytes 98308
Sparse Core Ops, SparseCore 0:
  64.7 68.8 reduce-scatter.1
  136.0 89.3 all-gather.2
where the time goes:
time: 245 us; the launch traced here: 244 us
  waiting for transfers between devices  124 us (51%)
  starting transfers between devices  41.9 us (17%)
  matrix products  20.8 us (8%)
  blocking collectives  19.2 us (8%)
  local copies, waits for them, and re-layouts  18.1 us (7%)
  between operations  15.6 us (6%)
  other arithmetic  4.45 us (2%)
    all_to_all x1, waiting for transfers between devices, body(): lax.all_to_all(tokens, 'dp', split_axis=1, concat_axis=0, tiled=True)  39.4 us
    all_to_all x1, waiting for transfers between devices, body(): lax.all_to_all(slice_grads, 'dp', split_axis=0, concat_axis=2, tiled=True)  30.1 us
    all_gather x1, waiting for transfers between devices, body(): weight_rows = lax.all_gather(base_weight, 'dp', axis=0, tiled=True)  29.8 us
    all_gather x1, blocking collectives, body(): rank_all = lax.all_gather(backward_rank, 'dp', axis=0, tiled=True)  19.2 us
    all_to_all x1, starting transfers between devices, body(): lax.all_to_all(up_terms.reshape(tiles_dev, -1), 'dp', split_axis=1, conca...  18.7 us
    reduce_scatter x1, waiting for transfers between devices, body(): lax.psum_scatter(jnp.einsum('tsd,trd->tsr', slice_tiles, down_all, prefer...  15 us
    all_to_all x1, starting transfers between devices, body(): lax.all_to_all(adapter_up[all_ids], 'dp', split_axis=0, concat_axis=1, ti...  11.2 us
    unnamed x27, local copies, waits for them, and re-layouts  11 us
  transfers between devices with their start and end apart: 6, of which 6 were waited for; matrix products, arithmetic and copies ran while one was open for 9% of the time, Pallas kernels for 0%

commit v1 on v0

v1 whole, which is shorter than its diff:
```python
import jax
import jax.numpy as jnp
from jax import lax
from jax.sharding import PartitionSpec as P

RANK_TILE = 16


def body(tokens, out_grad, base_weight, adapter_down, adapter_up, rank_tiles, tile_adapter):
    rows, model_width = tokens.shape
    out_width = out_grad.shape[1]
    adapters, rank_width, slice_width = adapter_down.shape
    all_ids = tile_adapter[:, 0]
    tiles = all_ids.shape[0]
    position = lax.axis_index("dp")
    holder = jnp.argsort(all_ids)
    my_tiles = rank_tiles[all_ids[position]]
    columns = jnp.arange(rank_width, dtype=jnp.int32)
    factor = jnp.where(columns < my_tiles * RANK_TILE, 2.0 / my_tiles.astype(jnp.float32), 0.0)

    weight = lax.all_gather(base_weight, "dp", axis=0, tiled=True)
    up_mine = lax.all_to_all(adapter_up[all_ids], "dp", split_axis=0, concat_axis=0, tiled=True)
    up_mine = up_mine.reshape(out_width, rank_width)
    down_mine = lax.all_to_all(adapter_down[all_ids], "dp", split_axis=0, concat_axis=0, tiled=True)

    backward = jnp.dot(out_grad, up_mine, preferred_element_type=jnp.float32)
    backward = (backward * factor[None, :]).astype(jnp.bfloat16)
    token_cols = tokens.reshape(rows, tiles, slice_width)
    down_term = jnp.einsum("sr,std->trd", backward, token_cols, preferred_element_type=jnp.float32)
    down_back = lax.all_to_all(
        down_term.astype(jnp.bfloat16), "dp", split_axis=0, concat_axis=0, tiled=True
    )
    down_grad = down_back[holder]

    lowrank = jnp.einsum("std,trd->sr", token_cols, down_mine, preferred_element_type=jnp.float32)
    hidden = (lowrank * factor[None, :]).astype(jnp.bfloat16)
    up_term = jnp.dot(out_grad.T, hidden, preferred_element_type=jnp.float32).astype(jnp.bfloat16)
    up_back = lax.all_to_all(
        up_term.reshape(tiles, -1), "dp", split_axis=0, concat_axis=0, tiled=True
    )
    up_grad = up_back[holder]
    out_low = jnp.dot(hidden, up_mine.T, preferred_element_type=jnp.float32)
    in_low = jnp.einsum("sr,trd->std", backward, down_mine, preferred_element_type=jnp.float32)
    in_low = in_low.astype(jnp.bfloat16).reshape(rows, model_width)

    forward = jnp.dot(tokens, weight, preferred_element_type=jnp.float32)
    grad_cols = jnp.dot(out_grad, weight.T, preferred_element_type=jnp.float32)
    result = (forward + out_low).astype(jnp.bfloat16)
    grad_in = (grad_cols + in_low.astype(jnp.float32)).astype(jnp.bfloat16)
    return result, grad_in, down_grad, up_grad


def solution(mesh):
    return jax.shard_map(
        body,
        mesh=mesh,
        in_specs=(
            P(("groups", "dp"), None),
            P(("groups", "dp"), None),
            P("dp", None),
            P(None, None, "dp"),
            P(None, "dp"),
            P(),
            P("groups", None),
        ),
        out_specs=(
            P(("groups", "dp"), None),
            P(("groups", "dp"), None),
            P("groups", None, "dp"),
            P("groups", "dp"),
        ),
        check_vma=False,
    )
```

time: 245 us -> 143 us (0.58)
  waiting for transfers between devices: 124 us -> 59.5 us
  blocking collectives: 19.2 us -> 0 us
  starting transfers between devices: 41.9 us -> 26.7 us
  matrix products: 20.8 us -> 16.2 us
    all_gather x1, waiting for transfers between devices: 29.8 us -> 0.01 us  [body(): weight = lax.all_gather(base_weight, 'dp', axis=0, tiled=True)]
    all_to_all x4, waiting for transfers between devices: 78.8 us -> 58.8 us  [the longest x1 25.3 us: body(): lax.all_to_all(adapter_down[all_ids], 'dp', split_axis=0, concat_axis=0,...]
    all_gather x1 -> x0, blocking collectives: 19.2 us -> none  [body(): rank_all = lax.all_gather(backward_rank, 'dp', axis=0, tiled=True)]
    all_to_all x4, starting transfers between devices: 41.9 us -> 26.6 us  [the longest x1 10.5 us: body(): lax.all_to_all(up_term.reshape(tiles, -1), 'dp', split_axis=0, concat_axi...]
    reduce_scatter x1 -> x0, waiting for transfers between devices: 15 us -> none  [body(): lax.psum_scatter(jnp.einsum('tsd,trd->tsr', slice_tiles, down_all, prefer...]
    unnamed x27 -> x29, local copies, waits for them, and re-layouts: 11 us -> 3.53 us
    dot_general x10 -> x8, matrix products: 20.8 us -> 16.2 us  [the longest x1 4.78 us: body(): forward = jnp.dot(tokens, weight, preferred_element_type=jnp.float32)]
    gather x1 -> x3, local copies, waits for them, and re-layouts: 1.58 us -> 5.62 us  [the longest x1 2.81 us: body(): down_grad = down_back[holder]]
  transfers between devices with their start and end apart: 6 -> 5, of which waited for: 6 -> 4; matrix products, arithmetic and copies ran while one was open for 9% -> 17% of each run, Pallas kernels for 0% -> 0%
where the time goes in v1:
time: 143 us; the launch traced here: 140 us
  waiting for transfers between devices  59.5 us (42%)
  starting transfers between devices  26.7 us (19%)
  between operations  17.6 us (12%)
  local copies, waits for them, and re-layouts  16.3 us (11%)
  matrix products  16.2 us (11%)
  other arithmetic  4.03 us (3%)
    all_to_all x1, waiting for transfers between devices, body(): lax.all_to_all(adapter_down[all_ids], 'dp', split_axis=0, concat_axis=0,...  25.3 us
    all_to_all x1, waiting for transfers between devices, body(): lax.all_to_all(down_term.astype(jnp.bfloat16), 'dp', split_axis=0, concat...  21.4 us
    all_to_all x1, starting transfers between devices, body(): lax.all_to_all(up_term.reshape(tiles, -1), 'dp', split_axis=0, concat_axi...  10.5 us
    all_to_all x1, starting transfers between devices, body(): lax.all_to_all(adapter_up[all_ids], 'dp', split_axis=0, concat_axis=0, ti...  7.39 us
    all_to_all x1, waiting for transfers between devices, body(): lax.all_to_all(up_term.reshape(tiles, -1), 'dp', split_axis=0, concat_axi...  6.84 us
    all_to_all x1, waiting for transfers between devices, body(): lax.all_to_all(adapter_up[all_ids], 'dp', split_axis=0, concat_axis=0, ti...  5.28 us
    dot_general x1, matrix products, body(): forward = jnp.dot(tokens, weight, preferred_element_type=jnp.float32)  4.78 us
    all_to_all x1, starting transfers between devices, body(): lax.all_to_all(down_term.astype(jnp.bfloat16), 'dp', split_axis=0, concat...  4.35 us
  transfers between devices with their start and end apart: 5, of which 4 were waited for; matrix products, arithmetic and copies ran while one was open for 17% of the time, Pallas kernels for 0%

profile of v1, /device:TPU:0, one launch (start us, length us, event | category | flops | bytes accessed | tf_op | source)
XLA Modules:
  0.0 140.3 jit_solution(1494985035477609364)
XLA Ops:
  7.2 0.0 copy-start
  7.2 0.0 all-gather.2.cloned.1.call-start
  7.2 0.7 all-gather.2.cloned.1.call-update
  7.9 0.7 fusion.26
  8.6 1.5 %gather_fusion.1 = bf16[16,2048]{1,0:T(8,128)(2,1)S(1)} fusion(bf16[16,2048]{1,0:T(8,128)(2,1)} %param.11, s32[1024]{0:T(1024)S(1)} %pad_clamp_fusion.1), kind=kCustom, calls=%fused_computation.1 | custom fusion | bytes 131136 | tf_op jit(solution)/shard_map/gather | solution.py:22
  10.1 0.6 broadcast.47
  10.7 0.7 reduce.1
  11.4 0.7 reshape.76
  12.1 7.4 %all-to-all-start.1 = ((bf16[16,2,1024]{2,1,0:T(2,128)(2,1)}), bf16[16,2,1024]{2,1,0:T(2,128)(2,1)S(1)}, u32[]{:S(2)}, u32[]{:S(2)}) async-start(bf16[16,2,1024]{2,1,0:T(2,128)(2,1)} %reshape.76), calls=%async_computation.1 | async-start | bytes 131072 | tf_op jit(solution)/shard_map/all_to_all | solution.py:22
  19.4 0.0 copy-done
  19.5 0.0 copy-start.10
  19.5 0.0 copy-start.9
  19.5 0.0 copy-start.4
  19.5 0.0 copy-start.3
  19.5 1.6 %gather_fusion = bf16[16,64,512]{2,1,0:T(8,128)(2,1)} fusion(bf16[16,64,512]{2,1,0:T(8,128)(2,1)S(1)} %copy-done, s32[1024]{0:T(1024)S(1)} %pad_clamp_fusion.1), kind=kCustom, calls=%fused_computation | custom fusion | bytes 2097216 | tf_op jit(solution)/shard_map/gather | solution.py:24
  21.1 5.3 %all-to-all-done.1 = bf16[16,2,1024]{2,1,0:T(2,128)(2,1)S(1)} async-done(((bf16[16,2,1024]{2,1,0:T(2,128)(2,1)}), bf16[16,2,1024]{2,1,0:T(2,128)(2,1)S(1)}, u32[]{:S(2)}, u32[]{:S(2)}) %all-to-all-start.1) | async-done | bytes 65568 | tf_op jit(solution)/shard_map/all_to_all | solution.py:22
  26.4 4.4 %all-to-all-start = ((bf16[16,64,512]{2,1,0:T(8,128)(2,1)}), bf16[16,64,512]{2,1,0:T(8,128)(2,1)}, u32[]{:S(2)}, u32[]{:S(2)}) async-start(bf16[16,64,512]{2,1,0:T(8,128)(2,1)} %gather_fusion), calls=%async_computation | async-start | bytes 2097152 | tf_op jit(solution)/shard_map/all_to_all | solution.py:24
  30.7 0.0 copy-done.10
  30.7 0.6 constant_dynamic-slice_fusion
  33.3 0.0 copy-done.9
  33.3 0.6 dynamic_slice.7
  35.2 0.1 reshape.77
  35.3 0.4 reduce
  35.6 0.2 reshape.37
  35.8 0.0 copy-done.4
  35.8 0.0 copy-start.5
  35.8 0.2 fusion.25
  36.0 25.3 %all-to-all-done = bf16[16,64,512]{2,1,0:T(8,128)(2,1)} async-done(((bf16[16,64,512]{2,1,0:T(8,128)(2,1)}), bf16[16,64,512]{2,1,0:T(8,128)(2,1)}, u32[]{:S(2)}, u32[]{:S(2)}) %all-to-all-start) | async-done | bytes 1048608 | tf_op jit(solution)/shard_map/all_to_all | solution.py:24
  61.3 0.0 copy-done.3
  61.3 2.1 %fusion.21 = bf16[64,128]{1,0:T(8,128)(2,1)S(1)} fusion(bf16[16,64,512]{2,1,0:T(8,128)(2,1)} %all-to-all-done, bf16[16,16,8,512]{3,2,1,0:T(8,128)(2,1)S(1)} %bitcast.56, f32[64]{0:T(128)S(1)} %compare_select_fusion.2), kind=kOutput, calls=%fused_computation.22 | convolution fusion | flops 134234112 | bytes 3162368 | tf_op jit(solution)/shard_map/std,trd->sr/dot_general | solution.py:35
  63.4 0.0 copy-start.7
  63.4 0.6 copy-done.7
  64.0 0.8 fusion.14
  64.8 0.0 copy-done.5
  64.8 1.0 copy.28
  65.7 0.1 all_to_all.27
  65.9 1.0 reduce.2
  66.9 0.7 reshape.78
  67.6 10.5 %all-to-all-start.3 = ((bf16[16,2,1024]{2,1,0:T(2,128)(2,1)}), bf16[16,2,1024]{2,1,0:T(2,128)(2,1)S(1)}, u32[]{:S(2)}, u32[]{:S(2)}) async-start(bf16[16,2,1024]{2,1,0:T(2,128)(2,1)} %reshape.78), calls=%async_computation.3 | async-start | bytes 131072 | tf_op jit(solution)/shard_map/all_to_all | solution.py:38
  78.1 0.0 copy-start.11
  78.1 1.4 %fusion.10 = bf16[16,64,512]{2,1,0:T(8,128)(2,1)} fusion(bf16[64,128,1]{1,0,2:T(8,128)(2,1)S(1)} %fusion.25, bf16[16,16,8,512]{3,2,1,0:T(8,128)(2,1)S(1)} %bitcast.57), kind=kOutput, calls=%fused_computation.14 | convolution fusion | flops 134742016 | bytes 3162112 | tf_op jit(solution)/shard_map/sr,std->trd/dot_general | solution.py:29
  79.5 6.8 %all-to-all-done.3 = bf16[16,2,1024]{2,1,0:T(2,128)(2,1)S(1)} async-done(((bf16[16,2,1024]{2,1,0:T(2,128)(2,1)}), bf16[16,2,1024]{2,1,0:T(2,128)(2,1)S(1)}, u32[]{:S(2)}, u32[]{:S(2)}) %all-to-all-start.3) | async-done | bytes 65568 | tf_op jit(solution)/shard_map/all_to_all | solution.py:38
  86.4 4.4 %all-to-all-start.2 = ((bf16[16,64,512]{2,1,0:T(8,128)(2,1)}), bf16[16,64,512]{2,1,0:T(8,128)(2,1)}, u32[]{:S(2)}, u32[]{:S(2)}) async-start(bf16[16,64,512]{2,1,0:T(8,128)(2,1)} %fusion.10), calls=%async_computation.2 | async-start | bytes 2097152 | tf_op jit(solution)/shard_map/all_to_all | solution.py:30
  90.8 0.0 copy-done.11
  90.8 1.2 sort.17
  92.0 2.0 %convert_bitcast_fusion = f32[16,16,8,512]{3,2,1,0:T(8,128)S(1)} fusion(bf16[64,128,1]{1,0,2:T(8,128)(2,1)S(1)} %fusion.25, bf16[16,64,512]{2,1,0:T(8,128)(2,1)} %all-to-all-done), kind=kOutput, calls=%fused_computation.6 | convolution fusion | flops 136314880 | bytes 5259264 | tf_op jit(solution)/shard_map/sr,trd->std/dot_general | solution.py:43
  94.0 2.6 %copy.32 = f32[16,16,8,512]{3,2,0,1:T(8,128)} copy(f32[16,16,8,512]{3,2,1,0:T(8,128)S(1)} %convert_bitcast_fusion) | data formatting | bytes 8388608 | tf_op jit(solution)/shard_map/convert_element_type | solution.py:49
  96.6 0.1 reshape.79
  96.7 1.2 gather_fusion.3
  97.9 21.4 %all-to-all-done.2 = bf16[16,64,512]{2,1,0:T(8,128)(2,1)} async-done(((bf16[16,64,512]{2,1,0:T(8,128)(2,1)}), bf16[16,64,512]{2,1,0:T(8,128)(2,1)}, u32[]{:S(2)}, u32[]{:S(2)}) %all-to-all-start.2) | async-done | bytes 1048608 | tf_op jit(solution)/shard_map/all_to_all | solution.py:30
  119.3 2.8 %gather_fusion.2 = bf16[16,64,512]{2,1,0:T(8,128)(2,1)} fusion(bf16[16,64,512]{2,1,0:T(8,128)(2,1)} %all-to-all-done.2, s32[1024]{0:T(1024)S(1)} %pad_clamp_fusion), kind=kCustom, calls=%fused_computation.2 | custom fusion | bytes 2097216 | tf_op jit(solution)/shard_map/gather | solution.py:33
  122.2 0.0 copy-start.6
  122.2 0.0 copy-start.8
  122.2 0.0 all-gather.2.cloned.1.call-done
  122.2 0.0 copy-start.1
  122.2 0.0 copy-start.2
  122.2 4.8 %fusion.27 = f32[128,512]{1,0:T(8,128)S(1)} fusion(bf16[128,8192]{1,0:T(8,128)(2,1)S(1)} %copy-done.3, bf16[8192,512]{1,0:T(8,128)(2,1)} %all-gather.2.cloned.1.call-done), kind=kOutput, calls=%fused_computation.33 | convolution fusion | flops 1073741824 | bytes 10747904 | tf_op jit(solution)/shard_map/dot_general | solution.py:46
  127.0 0.0 copy-done.6
  127.0 0.0 copy-done.8
  127.0 0.9 fusion.13
  127.9 0.2 copy-done.1
  128.0 1.2 copy-done.2
  129.3 4.2 %fusion = bf16[128,8192]{1,0:T(8,128)(2,1)} fusion(f32[128,8192]{1,0:T(8,128)S(1)} %bitcast.55, bf16[128,512]{1,0:T(8,128)(2,1)S(1)} %copy-done.4, bf16[8192,512]{1,0:T(8,128)(2,1)S(1)} %copy-done.1), kind=kOutput, calls=%fused_computation.5 | convolution fusion | flops 1075838976 | bytes 14811136 | tf_op jit(solution)/shard_map/dot_general | solution.py:47
  (6 shorter events, 0.1 us)
Async XLA Ops:
  7.2 12.3 %copy-start = (bf16[16,64,512]{2,1,0:T(8,128)(2,1)S(1)}, bf16[16,64,512]{2,1,0:T(8,128)(2,1)}, u32[]{:S(2)}) copy-start(bf16[16,64,512]{2,1,0:T(8,128)(2,1)} %param.10) | copy-start | bytes 3145732
  7.2 115.0 %all-gather.2.cloned.1.call-start = ((), (), s32[]{:S(2)}) async-start(), calls=%async_computation.4 | async-start | bytes 8912896 | tf_op jit(solution)/shard_map/all_gather | solution.py:21
  12.1 14.3 %all-to-all-start.1 = ((bf16[16,2,1024]{2,1,0:T(2,128)(2,1)}), bf16[16,2,1024]{2,1,0:T(2,128)(2,1)S(1)}, u32[]{:S(2)}, u32[]{:S(2)}) async-start(bf16[16,2,1024]{2,1,0:T(2,128)(2,1)} %reshape.76), calls=%async_computation.1 | async-start | bytes 131072 | tf_op jit(solution)/shard_map/all_to_all | solution.py:22
  19.5 11.3 %copy-start.10 = (s32[16,1]{0,1:T(1,128)S(1)}, s32[16,1]{0,1:T(1,128)}, u32[]{:S(2)}) copy-start(s32[16,1]{0,1:T(1,128)} %param.13) | copy-start | bytes 196
  19.5 13.8 %copy-start.9 = (s32[16]{0:T(128)S(1)}, s32[16]{0:T(128)}, u32[]{:S(2)}) copy-start(s32[16]{0:T(128)} %param.12) | copy-start | bytes 196
  19.5 16.3 %copy-start.4 = (bf16[128,512]{1,0:T(8,128)(2,1)S(1)}, bf16[128,512]{1,0:T(8,128)(2,1)}, u32[]{:S(2)}) copy-start(bf16[128,512]{1,0:T(8,128)(2,1)} %param.8) | copy-start | bytes 393220
  19.5 41.8 %copy-start.3 = (bf16[128,8192]{1,0:T(8,128)(2,1)S(1)}, bf16[128,8192]{1,0:T(8,128)(2,1)}, u32[]{:S(2)}) copy-start(bf16[128,8192]{1,0:T(8,128)(2,1)} %param.7) | copy-start | bytes 6291460
  26.4 34.9 %all-to-all-start = ((bf16[16,64,512]{2,1,0:T(8,128)(2,1)}), bf16[16,64,512]{2,1,0:T(8,128)(2,1)}, u32[]{:S(2)}, u32[]{:S(2)}) async-start(bf16[16,64,512]{2,1,0:T(8,128)(2,1)} %gather_fusion), calls=%async_computation | async-start | bytes 2097152 | tf_op jit(solution)/shard_map/all_to_all | solution.py:24
  35.8 28.9 %copy-start.5 = (bf16[512,64]{1,0:T(8,128)(2,1)}, bf16[512,64]{1,0:T(8,128)(2,1)S(1)}, u32[]{:S(2)}) copy-start(bf16[512,64]{1,0:T(8,128)(2,1)S(1)} %reshape.37) | copy-start | bytes 196612
  63.4 0.6 copy-start.7
  67.6 18.8 %all-to-all-start.3 = ((bf16[16,2,1024]{2,1,0:T(2,128)(2,1)}), bf16[16,2,1024]{2,1,0:T(2,128)(2,1)S(1)}, u32[]{:S(2)}, u32[]{:S(2)}) async-start(bf16[16,2,1024]{2,1,0:T(2,128)(2,1)} %reshape.78), calls=%async_computation.3 | async-start | bytes 131072 | tf_op jit(solution)/shard_map/all_to_all | solution.py:38
  78.1 12.6 %copy-start.11 = (s32[16,1]{0,1:T(1,128)S(1)}, s32[16,1]{0,1:T(1,128)}, u32[]{:S(2)}) copy-start(s32[16,1]{0,1:T(1,128)} %param.13) | copy-start | bytes 196
  86.4 33.0 %all-to-all-start.2 = ((bf16[16,64,512]{2,1,0:T(8,128)(2,1)}), bf16[16,64,512]{2,1,0:T(8,128)(2,1)}, u32[]{:S(2)}, u32[]{:S(2)}) async-start(bf16[16,64,512]{2,1,0:T(8,128)(2,1)} %fusion.10), calls=%async_computation.2 | async-start | bytes 2097152 | tf_op jit(solution)/shard_map/all_to_all | solution.py:30
  122.2 4.8 %copy-start.6 = (bf16[512,64]{1,0:T(8,128)(2,1)S(1)}, bf16[512,64]{1,0:T(8,128)(2,1)}, u32[]{:S(2)}) copy-start(bf16[512,64]{1,0:T(8,128)(2,1)} %copy-done.5) | copy-start | bytes 196612
  122.2 4.8 %copy-start.8 = (bf16[64,128]{1,0:T(8,128)(2,1)S(1)}, bf16[64,128]{1,0:T(8,128)(2,1)}, u32[]{:S(2)}) copy-start(bf16[64,128]{1,0:T(8,128)(2,1)} %copy-done.7) | copy-start | bytes 49156
  122.2 5.9 %copy-start.1 = (bf16[8192,512]{1,0:T(8,128)(2,1)S(1)}, bf16[8192,512]{1,0:T(8,128)(2,1)}, u32[]{:S(2)}) copy-start(bf16[8192,512]{1,0:T(8,128)(2,1)} %all-gather.2.cloned.1.call-done) | copy-start | bytes 25165828
  122.2 7.1 %copy-start.2 = (f32[16,16,8,512]{3,2,0,1:T(8,128)S(1)}, f32[16,16,8,512]{3,2,0,1:T(8,128)}, u32[]{:S(2)}) copy-start(f32[16,16,8,512]{3,2,0,1:T(8,128)} %copy.32) | copy-start | bytes 12582916
Sparse Core Ops, SparseCore 0:
  10.2 107.3 all-gather.1

commit v2 on v1

v2 whole, which is shorter than its diff:
```python
import functools

import jax
import jax.numpy as jnp
from jax import lax
from jax.experimental import pallas as pl
from jax.experimental.pallas import tpu as pltpu
from jax.sharding import PartitionSpec as P

RANK_TILE = 16
AXES = ("groups", "dp")
F32 = jnp.float32
BF16 = jnp.bfloat16
VMEM = pl.BlockSpec(memory_space=pltpu.VMEM)
SMEM = pl.BlockSpec(memory_space=pltpu.SMEM)


def dot(a, b, ca, cb):
    return lax.dot_general(a, b, (((ca,), (cb,)), ((), ())), preferred_element_type=F32)


def call(kernel, outs, scalars, arrays, flops=0):
    size = sum(x.size * x.dtype.itemsize for x in arrays)
    size += sum(x.size * x.dtype.itemsize for x in outs)
    return pl.pallas_call(
        kernel,
        out_shape=outs,
        in_specs=[SMEM] * len(scalars) + [VMEM] * len(arrays),
        out_specs=[VMEM] * len(outs),
        compiler_params=pltpu.CompilerParams(vmem_limit_bytes=40 * 1024 * 1024),
        cost_estimate=pl.CostEstimate(flops=flops, bytes_accessed=size, transcendentals=0),
    )(*scalars, *arrays)


def shape(dims, dtype=BF16):
    return jax.ShapeDtypeStruct(dims, dtype)


def iota(dims, axis):
    return lax.broadcasted_iota(jnp.int32, dims, axis)


def factor_of(ids, ranks, tile, width):
    count = ranks[ids[tile]]
    scale = 2.0 / jnp.full((1, width), count, jnp.int32).astype(F32)
    return jnp.where(iota((1, width), 1) < count * RANK_TILE, scale, 0.0)


def pack_kernel(chips, meta, ids, down, up_own, up_other, *blocks):
    adapters, rank, width = down.shape
    k, c = meta[0], meta[1]
    rows = chips * 16
    q = iota((rows, adapters), 0)
    chosen = jnp.zeros((rows, adapters), jnp.int32)
    for j in range(chips):
        for slot in range(2):
            adapter = ids[2 * jnp.bitwise_xor(k, j) + jnp.bitwise_xor(c, slot)]
            blocks[j][rank * slot : rank * (slot + 1), :] = down[adapter]
            chosen = jnp.where(q // 8 == 2 * j + slot, adapter, chosen)
    match = chosen == iota((rows, adapters), 1)
    packed = jnp.zeros((rows, width), F32)
    for side, up in enumerate((up_own, up_other)):
        for r in range(4):
            pick = (match & (q % 8 == 4 * side + r)).astype(F32).astype(BF16)
            packed = packed + dot(pick, up[:, width * r : width * (r + 1)], 1, 0)
    packed = packed.astype(BF16)
    for j in range(chips):
        blocks[j][2 * rank : 2 * rank + 16, :] = packed[16 * j : 16 * (j + 1), :]


def rank_kernel(chips, meta, ids, ranks, tok_own, tok_sib, og_own, og_sib, *refs):
    blocks, outs = refs[:chips], refs[chips:]
    grads, (low_own, low_sib, back_own, back_sib, up_out) = outs[:chips], outs[chips:]
    width = blocks[0].shape[1]
    out_width = og_own.shape[1]
    rank = back_own.shape[1]
    k, c = meta[0], meta[1]
    heads = out_width // (2 * chips)
    per_row = width // rank
    packed = jnp.concatenate([b[2 * rank : 2 * rank + 16, :] for b in blocks], axis=0)
    q = iota((out_width, chips * 16), 1)
    o = iota((out_width, chips * 16), 0)
    device = 2 * jnp.bitwise_xor(k, q // 16) + jnp.bitwise_xor(c, (q // 4) % 2)
    place = o // per_row == device * (heads // per_row) + q % 4
    lane_ok = iota((out_width, width), 1) // rank == iota((out_width, width), 0) % per_row
    fold = (iota((width, rank), 0) % rank == iota((width, rank), 1)).astype(F32).astype(BF16)
    for slot, (tok, og, low, back) in enumerate(
        ((tok_own, og_own, low_own, back_own), (tok_sib, og_sib, low_sib, back_sib))
    ):
        pick = (place & ((q // 8) % 2 == slot)).astype(F32).astype(BF16)
        spread = jnp.where(lane_ok, dot(pick, packed, 1, 0), 0.0).astype(BF16)
        up = dot(spread, fold, 1, 0).astype(BF16)
        if slot == 0:
            up_out[...] = up
        factor = factor_of(ids, ranks, 2 * k + jnp.bitwise_xor(c, slot), rank)
        backward = (dot(og[...], up, 1, 0) * factor).astype(BF16)
        back[...] = backward
        turned = backward.T
        total = jnp.zeros((tok.shape[0], rank), F32)
        for j in range(chips):
            start = pl.multiple_of((2 * jnp.bitwise_xor(k, j) + c) * width, width)
            part = tok[:, pl.ds(start, width)]
            grads[j][rank * slot : rank * (slot + 1), :] = dot(turned, part, 1, 0).astype(BF16)
            total = total + dot(part, blocks[j][rank * slot : rank * (slot + 1), :], 1, 1)
        low[...] = total


def hidden_kernel(meta, ids, ranks, low_mine, low_other, og, up, up_term, out_low):
    rank = up.shape[1]
    out_width = og.shape[1]
    factor = factor_of(ids, ranks, 2 * meta[0] + meta[1], rank)
    hidden = ((low_mine[...] + low_other[...]) * factor).astype(BF16)
    out_low[...] = dot(hidden, up[...], 1, 1)
    term = dot(og[...], hidden, 0, 0).astype(BF16)
    half = out_width // 2
    total = jnp.zeros((half, 2 * rank), F32)
    for odd in range(2):
        pick = (iota((half, out_width), 1) == 2 * iota((half, out_width), 0) + odd)
        move = (iota((rank, 2 * rank), 1) == iota((rank, 2 * rank), 0) + odd * rank)
        rows = dot(pick.astype(F32).astype(BF16), term, 1, 0).astype(BF16)
        total = total + dot(rows, move.astype(F32).astype(BF16), 1, 0)
    up_term[...] = total.astype(BF16).reshape(up_term.shape)


def base_kernel(chips, plan, meta, tok_own, tok_sib, og_own, og_sib, back_own, back_sib, *refs):
    blocks = refs[:chips]
    pieces = refs[chips : len(refs) - 4]
    for_own, for_sib, grad_own, grad_sib = refs[len(refs) - 4 :]
    width = blocks[0].shape[1]
    rank = back_own.shape[1]
    rows = tok_own.shape[0]
    k, c, g = meta[0], meta[1], meta[2]
    og = jnp.concatenate([og_own[...], og_sib[...]], axis=0)
    total = jnp.zeros((2 * rows, og.shape[1]), F32)
    for piece, (j, count, side, whole) in zip(pieces, plan):
        chip = jnp.bitwise_xor(k, j)
        shift = 0 if side is None else jnp.bitwise_xor(g, side) * count
        if whole:
            weight = piece[pl.ds(pl.multiple_of(chip * count, count), count), :]
        else:
            weight = piece[...]
        start = pl.multiple_of((2 * chip + c) * width + shift, 128)
        tok = jnp.concatenate(
            [tok_own[:, pl.ds(start, count)], tok_sib[:, pl.ds(start, count)]], axis=0
        )
        total = total + dot(tok, weight, 1, 0)
        grad = dot(og, weight, 1, 1)
        inner = pl.ds(pl.multiple_of(shift, 128), count)
        low_own = dot(back_own[...], blocks[j][0:rank, inner], 1, 0).astype(BF16)
        low_sib = dot(back_sib[...], blocks[j][rank : 2 * rank, inner], 1, 0).astype(BF16)
        to = pl.ds(pl.multiple_of(chip * width + shift, 128), count)
        grad_own[:, to] = (grad[:rows] + low_own.astype(F32)).astype(BF16)
        grad_sib[:, to] = (grad[rows:] + low_sib.astype(F32)).astype(BF16)
    for_own[...] = total[:rows]
    for_sib[...] = total[rows:]


def join_kernel(chips, meta, mine, other, out_low, grad_mine, grad_other, result, grad_in):
    c = meta[1]
    result[...] = (mine[...] + other[...] + out_low[...]).astype(BF16)
    width = grad_mine.shape[1] // chips
    for chip in range(chips):
        cols = slice(width * chip, width * (chip + 1))
        own = pl.multiple_of((2 * chip + c) * width, width)
        sib = pl.multiple_of((2 * chip + 1 - c) * width, width)
        grad_in[:, pl.ds(own, width)] = grad_mine[:, cols]
        grad_in[:, pl.ds(sib, width)] = grad_other[:, cols]


def down_kernel(chips, meta, ids, *refs):
    out = refs[-1]
    rank = out.shape[1]
    k, c = meta[0], meta[1]
    for j in range(chips):
        for slot in range(2):
            adapter = ids[2 * jnp.bitwise_xor(k, j) + jnp.bitwise_xor(c, slot)]
            out[adapter] = refs[j][rank * slot : rank * (slot + 1), :]


def up_kernel(ids, back, out):
    tiles, rows, lanes = back.shape
    flat = back[...].reshape(tiles * rows, lanes)
    q = iota((out.shape[0], tiles * rows), 1)
    chosen = jnp.zeros(q.shape, jnp.int32)
    for tile in range(tiles):
        chosen = jnp.where(q // rows == tile, ids[tile], chosen)
    match = chosen == iota(q.shape, 0)
    for row in range(rows):
        pick = (match & (q % rows == row)).astype(F32).astype(BF16)
        out[:, lanes * row : lanes * (row + 1)] = dot(pick, flat, 1, 0).astype(BF16)


def pairs(groups, size, to):
    out = []
    for g in range(groups):
        for d in range(size):
            target = to(g, d)
            if target is not None:
                out.append((g * size + d, target[0] * size + target[1]))
    return out


def gather_weight(weight, groups, size, send):
    chips = size // 2
    rows = weight.shape[0]
    if groups != 2 or chips != 8:
        lists = [[2 * chip + core for chip in range(chips)] for core in range(2)]
        full = lax.all_gather(weight, "dp", axis=0, tiled=True, axis_index_groups=lists)
        return [(full, (j, rows, None, True)) for j in range(chips)]
    half = rows // 2
    place = lax.axis_index("dp")
    z = place // 4
    middle = (z == 1) | (z == 2)
    mine = lax.dynamic_slice_in_dim(weight, lax.axis_index("groups") * half, half)
    swap_x = lambda g, d: (1 - g, d)
    swap_y = lambda g, d: (g, d ^ 2)
    swap_near = lambda g, d: (g, d ^ 4)
    swap_mid = lambda g, d: (g, d ^ 12) if d // 4 in (1, 2) else None
    outward = lambda g, d: (g, d ^ 4) if d // 4 in (1, 2) else None
    near = send(mine, swap_near)
    cross = send(mine, swap_mid)
    own_y = send(weight, swap_y)
    cross_near = send(near, swap_mid)
    edge = send(cross, outward)
    edge_near = send(cross_near, outward)
    by_slot = (
        (2, near),
        (4, jnp.where(middle, cross_near, edge)),
        (6, jnp.where(middle, cross, edge_near)),
    )
    pieces = [(weight, (0, rows, None, False)), (own_y, (1, rows, None, False))]
    for j, held in by_slot:
        over_y = send(held, swap_y)
        pieces.append((held, (j, half, 0, False)))
        pieces.append((send(held, swap_x), (j, half, 1, False)))
        pieces.append((over_y, (j + 1, half, 0, False)))
        pieces.append((send(over_y, swap_x), (j + 1, half, 1, False)))
    return pieces


def body(groups, size, tokens, out_grad, base_weight, adapter_down, adapter_up, rank_tiles, tile_adapter):
    chips = size // 2
    rows, model_width = tokens.shape
    out_width = out_grad.shape[1]
    adapters, rank, width = adapter_down.shape
    ids = tile_adapter[:, 0]
    place = lax.axis_index("dp")
    meta = jnp.stack([place // 2, place % 2, lax.axis_index("groups")]).astype(jnp.int32)

    def send(x, to):
        return lax.ppermute(x, AXES, pairs(groups, size, to))

    def sibling(x):
        return send(x, lambda g, d: (g, d ^ 1))

    def exchange(blocks):
        moved = [blocks[0]] + [None] * (chips - 1)
        for j in reversed(range(1, chips)):
            moved[j] = send(blocks[j], lambda g, d: (g, d ^ (2 * j)))
        return moved

    up_sib = sibling(adapter_up)
    tok_sib = sibling(tokens)
    og_sib = sibling(out_grad)
    block = shape((2 * rank + 16, width))
    packed = call(
        functools.partial(pack_kernel, chips),
        [block] * chips,
        (meta, ids),
        (adapter_down, adapter_up, up_sib),
    )
    blocks = exchange(packed)
    pieces = gather_weight(base_weight, groups, size, send)

    *grads, low_own, low_sib, back_own, back_sib, up_mine = call(
        functools.partial(rank_kernel, chips),
        [shape((2 * rank, width))] * chips
        + [shape((rows, rank), F32)] * 2
        + [shape((rows, rank))] * 2
        + [shape((out_width, rank))],
        (meta, ids, rank_tiles),
        (tokens, tok_sib, out_grad, og_sib, *blocks),
        flops=4 * rows * model_width * rank,
    )
    grads_back = exchange(grads)
    low_other = sibling(low_sib)
    up_rows = adapter_up.shape[1] // (2 * rank)
    up_term, out_low = call(
        hidden_kernel,
        [shape((size, up_rows, 2 * rank)), shape((rows, out_width), F32)],
        (meta, ids, rank_tiles),
        (low_own, low_other, out_grad, up_mine),
        flops=4 * rows * out_width * rank,
    )
    up_back = lax.all_to_all(up_term, "dp", split_axis=0, concat_axis=0, tiled=True)
    (up_grad,) = call(up_kernel, [shape(adapter_up.shape)], (ids,), (up_back,))

    for_own, for_sib, grad_own, grad_sib = call(
        functools.partial(base_kernel, chips, [p[1] for p in pieces]),
        [shape((rows, out_width), F32)] * 2 + [shape((rows, model_width // 2))] * 2,
        (meta,),
        (tokens, tok_sib, out_grad, og_sib, back_own, back_sib, *blocks, *[p[0] for p in pieces]),
        flops=4 * rows * model_width * out_width,
    )
    for_other, grad_other = sibling(for_sib), sibling(grad_sib)
    result, grad_in = call(
        functools.partial(join_kernel, chips),
        [shape((rows, out_width)), shape((rows, model_width))],
        (meta,),
        (for_own, for_other, out_low, grad_own, grad_other),
    )
    (down_grad,) = call(
        functools.partial(down_kernel, chips),
        [shape(adapter_down.shape)],
        (meta, ids),
        tuple(grads_back),
    )
    return result, grad_in, down_grad, up_grad


def solution(mesh):
    return jax.shard_map(
        functools.partial(body, mesh.shape["groups"], mesh.shape["dp"]),
        mesh=mesh,
        in_specs=(
            P(("groups", "dp"), None),
            P(("groups", "dp"), None),
            P("dp", None),
            P(None, None, "dp"),
            P(None, "dp"),
            P(),
            P("groups", None),
        ),
        out_specs=(
            P(("groups", "dp"), None),
            P(("groups", "dp"), None),
            P("groups", None, "dp"),
            P("groups", "dp"),
        ),
        check_vma=False,
    )
```

time: 143 us -> 143 us (level)
  the two profiles are of different devices: /device:TPU:0 before, /device:TPU:11 now
where the time goes in v2:
time: 143 us; the launch traced here: 142 us
  starting transfers between devices  54.5 us (38%)
  waiting for transfers between devices  50.9 us (36%)
  Pallas kernels  19.7 us (14%)
  local copies, waits for them, and re-layouts  14.3 us (10%)
  other arithmetic  2.04 us (1%)
    ppermute x35, waiting for transfers between devices, send(): return lax.ppermute(x, AXES, pairs(groups, size, to))  50.9 us
    ppermute x35, starting transfers between devices, send(): return lax.ppermute(x, AXES, pairs(groups, size, to))  44.5 us
    pallas_call x7, Pallas kernels, call(): pl.pallas_call(kernel, out_shape=outs, in_specs=[SMEM] * len(scalars) + [...  19.7 us
    unnamed x72, local copies, waits for them, and re-layouts  13.3 us
    all_to_all x1, starting transfers between devices, body(): lax.all_to_all(up_term, 'dp', split_axis=0, concat_axis=0, tiled=True)  9.95 us
  transfers between devices with their start and end apart: 36, of which 19 were waited for; matrix products, arithmetic and copies ran while one was open for 2% of the time, Pallas kernels for 8%

profile of v2, /device:TPU:11, one launch (start us, length us, event | category | flops | bytes accessed | tf_op | source)
XLA Modules:
  0.0 142.2 jit_solution(3866655075513196887)
XLA Ops:
  0.7 0.7 collective-permute-start
  1.4 1.0 constant_dynamic-slice_fusion
  2.4 3.2 %collective-permute-start.16 = (bf16[256,512]{1,0:T(8,128)(2,1)S(1)}, bf16[256,512]{1,0:T(8,128)(2,1)}, u32[]{:S(2)}, u32[]{:S(2)}) collective-permute-start(bf16[256,512]{1,0:T(8,128)(2,1)S(1)} %constant_dynamic-slice_fusion), channel_id=1, source_target_pairs={{4,8},{5,9},{6,10},{7,11},{8,4},{9,5},{10,6},{11,7},{20,24},{21,25... | collective-permute-start | bytes 786440 | tf_op jit(solution)/shard_map/ppermute | solution.py:251
  6.2 1.0 collective-permute-done.2.up_other
  7.3 1.2 copy-done.3
  8.5 0.8 copy-done.22
  9.3 0.7 copy-done.27
  10.0 1.7 %shard_map.102 = (bf16[144,512]{1,0:T(8,128)(2,1)S(1)}, bf16[144,512]{1,0:T(8,128)(2,1)S(1)}, bf16[144,512]{1,0:T(8,128)(2,1)S(1)}, bf16[144,512]{1,0:T(8,128)(2...) custom-call(s32[3]{0:T(128)S(1)} %pad_add_fusion.meta, ...), custom_call_target="tpu_custom_call" | custom-call | bytes 2359296 | tf_op jit(solution)/shard_map/pallas_call | solution.py:25
  11.7 0.7 copy-done.35
  12.4 1.2 collective-permute-start.3
  13.6 0.6 collective-permute-start.1
  14.2 1.2 collective-permute-done.1.og_sib
  15.4 1.7 %collective-permute-start.4 = (bf16[144,512]{1,0:T(8,128)(2,1)S(1)}, bf16[144,512]{1,0:T(8,128)(2,1)S(1)}, u32[]{:S(2)}, u32[]{:S(2)}) collective-permute-start(bf16[144,512]{1,0:T(8,128)(2,1)S(1)} %get-tuple-element.35), channel_id=1, source_target_pairs={{0,4},{1,5},{2,6},{3,7},{4,0},{5,1},{6,2},{7,3},{8,12},{9,13},{10,... | collective-permute-start | bytes 442376 | tf_op jit(solution)/shard_map/ppermute | solution.py:251
  17.4 2.6 %collective-permute-start.5 = (bf16[144,512]{1,0:T(8,128)(2,1)S(1)}, bf16[144,512]{1,0:T(8,128)(2,1)S(1)}, u32[]{:S(2)}, u32[]{:S(2)}) collective-permute-start(bf16[144,512]{1,0:T(8,128)(2,1)S(1)} %get-tuple-element.36), channel_id=1, source_target_pairs={{0,6},{1,7},{2,4},{3,5},{4,2},{5,3},{6,0},{7,1},{8,14},{9,15},{10,... | collective-permute-start | bytes 442376 | tf_op jit(solution)/shard_map/ppermute | solution.py:251
  20.1 2.1 %collective-permute-start.15 = (bf16[256,512]{1,0:T(8,128)(2,1)S(1)}, bf16[256,512]{1,0:T(8,128)(2,1)}, u32[]{:S(2)}, u32[]{:S(2)}) collective-permute-start(bf16[256,512]{1,0:T(8,128)(2,1)S(1)} %collective-permute-done.11.refs_10_), channel_id=1, source_target_pairs={{4,8},{5,9},{6,10},{7,11},{8,4},{9,5},{10,6},{11,7},{20,24},{21,25... | collective-permute-start | bytes 786440 | tf_op jit(solution)/shard_map/ppermute | solution.py:251
  22.2 2.0 %collective-permute-start.17 = (bf16[256,512]{1,0:T(8,128)(2,1)}, bf16[256,512]{1,0:T(8,128)(2,1)}, u32[]{:S(2)}, u32[]{:S(2)}) collective-permute-start(bf16[256,512]{1,0:T(8,128)(2,1)} %collective-permute-done.16), channel_id=1, source_target_pairs={{4,0},{5,1},{6,2},{7,3},{8,12},{9,13},{10,14},{11,15},{20,16},{21,... | collective-permute-start | bytes 786440 | tf_op jit(solution)/shard_map/ppermute | solution.py:251
  24.2 2.3 %collective-permute-start.7 = (bf16[144,512]{1,0:T(8,128)(2,1)}, bf16[144,512]{1,0:T(8,128)(2,1)S(1)}, u32[]{:S(2)}, u32[]{:S(2)}) collective-permute-start(bf16[144,512]{1,0:T(8,128)(2,1)} %get-tuple-element.38), channel_id=1, source_target_pairs={{0,10},{1,11},{2,8},{3,9},{4,14},{5,15},{6,12},{7,13},{8,2},{9,3},... | collective-permute-start | bytes 442376 | tf_op jit(solution)/shard_map/ppermute | solution.py:251
  26.5 8.3 %collective-permute-done.15 = bf16[256,512]{1,0:T(8,128)(2,1)} collective-permute-done((bf16[256,512]{1,0:T(8,128)(2,1)S(1)}, bf16[256,512]{1,0:T(8,128)(2,1)}, u32[]{:S(2)}, u32[]{:S(2)}) %collective-permute-start.15) | collective-permute-done | bytes 262176 | tf_op jit(solution)/shard_map/ppermute | solution.py:251
  34.7 2.0 %collective-permute-start.21 = (bf16[256,512]{1,0:T(8,128)(2,1)}, bf16[256,512]{1,0:T(8,128)(2,1)}, u32[]{:S(2)}, u32[]{:S(2)}) collective-permute-start(bf16[256,512]{1,0:T(8,128)(2,1)} %collective-permute-done.15), channel_id=1, source_target_pairs={{4,0},{5,1},{6,2},{7,3},{8,12},{9,13},{10,14},{11,15},{20,16},{21,... | collective-permute-start | bytes 786440 | tf_op jit(solution)/shard_map/ppermute | solution.py:251
  37.0 2.0 %collective-permute-done.7.refs_5_ = bf16[144,512]{1,0:T(8,128)(2,1)S(1)} collective-permute-done((bf16[144,512]{1,0:T(8,128)(2,1)}, bf16[144,512]{1,0:T(8,128)(2,1)S(1)}, u32[]{:S(2)}, u32[]{:S(2)}) %collective-permute-start.7) | collective-permute-done | bytes 147488 | tf_op jit(solution)/shard_map/ppermute | solution.py:251
  39.0 1.3 collective-permute-start.8
  40.6 1.0 broadcast_select_fusion.1.refs_14_
  41.6 2.7 %collective-permute-done.8.refs_6_ = bf16[144,512]{1,0:T(8,128)(2,1)S(1)} collective-permute-done((bf16[144,512]{1,0:T(8,128)(2,1)}, bf16[144,512]{1,0:T(8,128)(2,1)S(1)}, u32[]{:S(2)}, u32[]{:S(2)}) %collective-permute-start.8) | collective-permute-done | bytes 147488 | tf_op jit(solution)/shard_map/ppermute | solution.py:251
  44.3 0.5 collective-permute-start.9
  44.8 3.3 %collective-permute-done.21 = bf16[256,512]{1,0:T(8,128)(2,1)} collective-permute-done((bf16[256,512]{1,0:T(8,128)(2,1)}, bf16[256,512]{1,0:T(8,128)(2,1)}, u32[]{:S(2)}, u32[]{:S(2)}) %collective-permute-start.21) | collective-permute-done | bytes 262176 | tf_op jit(solution)/shard_map/ppermute | solution.py:251
  48.4 1.0 broadcast_select_fusion.refs_18_
  49.3 2.8 %collective-permute-done.9.refs_7_ = bf16[144,512]{1,0:T(8,128)(2,1)S(1)} collective-permute-done((bf16[144,512]{1,0:T(8,128)(2,1)}, bf16[144,512]{1,0:T(8,128)(2,1)S(1)}, u32[]{:S(2)}, u32[]{:S(2)}) %collective-permute-start.9) | collective-permute-done | bytes 147488 | tf_op jit(solution)/shard_map/ppermute | solution.py:251
  52.1 0.6 collective-permute-start.19
  53.9 1.2 collective-permute-start.14
  55.1 7.0 %collective-permute-done.19.refs_16_ = bf16[256,512]{1,0:T(8,128)(2,1)S(1)} collective-permute-done((bf16[256,512]{1,0:T(8,128)(2,1)S(1)}, bf16[256,512]{1,0:T(8,128)(2,1)S(1)}, u32[]{:S(2)}, u32[]{:S(2)}) %collective-permute-start.19) | collective-permute-done | bytes 262176 | tf_op jit(solution)/shard_map/ppermute | solution.py:251
  62.3 5.4 %collective-permute-done.23.refs_20_ = bf16[256,512]{1,0:T(8,128)(2,1)S(1)} collective-permute-done((bf16[256,512]{1,0:T(8,128)(2,1)S(1)}, bf16[256,512]{1,0:T(8,128)(2,1)S(1)}, u32[]{:S(2)}, u32[]{:S(2)}) %collective-permute-start.23) | collective-permute-done | bytes 262176 | tf_op jit(solution)/shard_map/ppermute | solution.py:251
  67.9 1.2 collective-permute-start.24
  69.2 4.9 %shard_map.103 = (bf16[128,512]{1,0:T(8,128)(2,1)S(1)}, bf16[128,512]{1,0:T(8,128)(2,1)S(1)}, bf16[128,512]{1,0:T(8,128)(2,1)S(1)}, bf16[128,512]{1,0:T(8,128)(2...) custom-call(s32[3]{0:T(128)S(1)} %pad_add_fusion.meta, ...), custom_call_target="tpu_custom_call" | custom-call | flops 268435456 | bytes 6848512 | tf_op jit(solution)/shard_map/pallas_call | solution.py:25
  74.1 0.6 copy-done.18
  74.7 1.3 collective-permute-done.20.refs_17_
  76.1 5.6 %collective-permute-done.24.refs_21_ = bf16[256,512]{1,0:T(8,128)(2,1)S(1)} collective-permute-done((bf16[256,512]{1,0:T(8,128)(2,1)S(1)}, bf16[256,512]{1,0:T(8,128)(2,1)S(1)}, u32[]{:S(2)}, u32[]{:S(2)}) %collective-permute-start.24) | collective-permute-done | bytes 262176 | tf_op jit(solution)/shard_map/ppermute | solution.py:251
  81.7 0.9 copy-done.5
  82.6 0.9 copy-done.7
  83.5 0.9 copy-done.9
  84.4 0.9 copy-done.11
  85.3 0.9 copy-done.13
  86.2 0.9 copy-done.15
  87.2 0.6 copy-done.24
  87.8 5.6 %shard_map.104 = (f32[128,512]{1,0:T(8,128)S(1)}, f32[128,512]{1,0:T(8,128)}, bf16[128,4096]{1,0:T(8,128)(2,1)S(1)}, bf16[128,4096]{1,0:T(8,128)(2,1)}) custom-call(s32[3]{0:T(128)S(1)} %copy-done.24, bf16[128,8192]{1,0:T(8,128)(2,1)S(1)} %copy-done, bf16[128,8192]{1,0:T(8,128)(2,1)} %collective-permute-done.tok_sib, bf16[128,512]{1,0:T(8,128)(2,1)S(1)} %copy-done.1, ...), custom_call_target="tpu_custom_call" | custom-call | flops 2147483648 | bytes 12484608 | tf_op jit(solution)/shard_map/pallas_call | solution.py:25
  93.5 6.0 %collective-permute-start.27 = (bf16[128,4096]{1,0:T(8,128)(2,1)}, bf16[128,4096]{1,0:T(8,128)(2,1)S(1)}, u32[]{:S(2)}, u32[]{:S(2)}) collective-permute-start(bf16[128,4096]{1,0:T(8,128)(2,1)} %get-tuple-element.50), channel_id=1, source_target_pairs={{0,1},{1,0},{2,3},{3,2},{4,5},{5,4},{6,7},{7,6},{8,9},{9,8},{10,11... | collective-permute-start | bytes 3145736 | tf_op jit(solution)/shard_map/ppermute | solution.py:251
  99.5 0.6 collective-permute-start.28
  100.5 4.6 %collective-permute-start.29 = (bf16[128,512]{1,0:T(8,128)(2,1)S(1)}, bf16[128,512]{1,0:T(8,128)(2,1)S(1)}, u32[]{:S(2)}, u32[]{:S(2)}) collective-permute-start(bf16[128,512]{1,0:T(8,128)(2,1)S(1)} %get-tuple-element.55), channel_id=1, source_target_pairs={{0,4},{1,5},{2,6},{3,7},{4,0},{5,1},{6,2},{7,3},{8,12},{9,13},{10,... | collective-permute-start | bytes 393224 | tf_op jit(solution)/shard_map/ppermute | solution.py:251
  105.1 2.5 %collective-permute-start.31 = (bf16[128,512]{1,0:T(8,128)(2,1)S(1)}, bf16[128,512]{1,0:T(8,128)(2,1)S(1)}, u32[]{:S(2)}, u32[]{:S(2)}) collective-permute-start(bf16[128,512]{1,0:T(8,128)(2,1)S(1)} %get-tuple-element.57), channel_id=1, source_target_pairs={{0,8},{1,9},{2,10},{3,11},{4,12},{5,13},{6,14},{7,15},{8,0},{9,1},... | collective-permute-start | bytes 393224 | tf_op jit(solution)/shard_map/ppermute | solution.py:251
  107.6 1.0 collective-permute-start.25
  108.9 2.2 %collective-permute-start.32 = (bf16[128,512]{1,0:T(8,128)(2,1)}, bf16[128,512]{1,0:T(8,128)(2,1)}, u32[]{:S(2)}, u32[]{:S(2)}) collective-permute-start(bf16[128,512]{1,0:T(8,128)(2,1)} %get-tuple-element.58), channel_id=1, source_target_pairs={{0,10},{1,11},{2,8},{3,9},{4,14},{5,15},{6,12},{7,13},{8,2},{9,3},... | collective-permute-start | bytes 393224 | tf_op jit(solution)/shard_map/ppermute | solution.py:251
  111.1 2.3 %collective-permute-done.30.refs_3_ = bf16[128,512]{1,0:T(8,128)(2,1)S(1)} collective-permute-done((bf16[128,512]{1,0:T(8,128)(2,1)S(1)}, bf16[128,512]{1,0:T(8,128)(2,1)S(1)}, u32[]{:S(2)}, u32[]{:S(2)}) %collective-permute-start.30) | collective-permute-done | bytes 131104 | tf_op jit(solution)/shard_map/ppermute | solution.py:251
  113.8 0.5 collective-permute-done.31.refs_4_
  114.3 1.0 collective-permute-start.34
  115.3 1.9 %shard_map.105 = (bf16[16,16,128]{2,1,0:T(8,128)(2,1)}, f32[128,512]{1,0:T(8,128)S(1)}) custom-call(s32[3]{0:T(128)S(1)} %copy-done.24, s32[16]{0:T(128)S(1)} %bitcast.6, s32[16]{0:T(128)S(1)} %copy-done.33, f32[128,64]{1,0:T(8,128)S(1)} %get-tuple-element.45.low_mine, f32[128,64]{1,0:T(8,128)S(1)} %collective-permute-done.26.low_other, ...), custom_call_target="tpu_custom_call" | custom-call | flops 16777216 | bytes 589824 | tf_op jit(solution)/shard_map/pallas_call | solution.py:25
  117.2 10.0 %all-to-all-start = ((bf16[16,16,128]{2,1,0:T(8,128)(2,1)}), bf16[16,16,128]{2,1,0:T(8,128)(2,1)S(1)}, u32[]{:S(2)}, u32[]{:S(2)}) async-start(bf16[16,16,128]{2,1,0:T(8,128)(2,1)} %get-tuple-element.61), calls=%async_computation | async-start | bytes 131072 | tf_op jit(solution)/shard_map/all_to_all | solution.py:295
  127.2 1.8 %collective-permute-done.33.refs_6_ = bf16[128,512]{1,0:T(8,128)(2,1)} collective-permute-done((bf16[128,512]{1,0:T(8,128)(2,1)}, bf16[128,512]{1,0:T(8,128)(2,1)}, u32[]{:S(2)}, u32[]{:S(2)}) %collective-permute-start.33) | collective-permute-done | bytes 131104 | tf_op jit(solution)/shard_map/ppermute | solution.py:251
  128.9 4.5 %collective-permute-done.34.refs_7_ = bf16[128,512]{1,0:T(8,128)(2,1)} collective-permute-done((bf16[128,512]{1,0:T(8,128)(2,1)}, bf16[128,512]{1,0:T(8,128)(2,1)}, u32[]{:S(2)}, u32[]{:S(2)}) %collective-permute-start.34) | collective-permute-done | bytes 131104 | tf_op jit(solution)/shard_map/ppermute | solution.py:251
  133.5 0.9 copy-done.19
  134.4 0.9 copy-done.21
  135.3 0.6 copy-done.25
  135.9 0.7 copy-done.30
  136.6 2.1 %shard_map.107 = bf16[16,64,512]{2,1,0:T(8,128)(2,1)} custom-call(s32[3]{0:T(128)S(1)} %copy-done.25, s32[16]{0:T(128)S(1)} %bitcast.7, bf16[128,512]{1,0:T(8,128)(2,1)S(1)} %copy-done.19, bf16[128,512]{1,0:T(8,128)(2,1)S(1)} %collective-permute-done.28.refs_1_, bf16[128,512]{1,0:T(8,128)(2,1)S(1)} %collective-permute-done.29.refs_2_, ...), custom_call_target="tpu_custom_call" | custom-call | bytes 2097152 | tf_op jit(solution)/shard_map/pallas_call | solution.py:25
  138.7 1.4 %shard_map.108 = bf16[16,2048]{1,0:T(8,128)(2,1)} custom-call(s32[16]{0:T(128)S(1)} %bitcast.8, bf16[16,16,128]{2,1,0:T(8,128)(2,1)S(1)} %all-to-all-done.back), custom_call_target="tpu_custom_call" | custom-call | bytes 131072 | tf_op jit(solution)/shard_map/pallas_call | solution.py:25
  140.1 2.1 %shard_map.106 = (bf16[128,512]{1,0:T(8,128)(2,1)}, bf16[128,8192]{1,0:T(8,128)(2,1)}) custom-call(s32[3]{0:T(128)S(1)} %copy-done.26, f32[128,512]{1,0:T(8,128)S(1)} %copy-done.17, f32[128,512]{1,0:T(8,128)S(1)} %collective-permute-done.25.other, f32[128,512]{1,0:T(8,128)S(1)} %get-tuple-element.48.out_low, ...), custom_call_target="tpu_custom_call" | custom-call | bytes 5111808 | tf_op jit(solution)/shard_map/pallas_call | solution.py:25
  (91 shorter events, 4.5 us)
Async XLA Ops:
  0.6 68.5 %copy-start = (bf16[128,8192]{1,0:T(8,128)(2,1)S(1)}, bf16[128,8192]{1,0:T(8,128)(2,1)}, u32[]{:S(2)}) copy-start(bf16[128,8192]{1,0:T(8,128)(2,1)} %tok_own.3) | copy-start | bytes 6291460
  0.6 68.5 %copy-start.1 = (bf16[128,512]{1,0:T(8,128)(2,1)S(1)}, bf16[128,512]{1,0:T(8,128)(2,1)}, u32[]{:S(2)}) copy-start(bf16[128,512]{1,0:T(8,128)(2,1)} %og.1) | copy-start | bytes 393220
  0.7 67.3 %collective-permute-start = (bf16[128,8192]{1,0:T(8,128)(2,1)}, bf16[128,8192]{1,0:T(8,128)(2,1)}, u32[]{:S(2)}, u32[]{:S(2)}) collective-permute-start(bf16[128,8192]{1,0:T(8,128)(2,1)} %tok_own.3), channel_id=1, source_target_pairs={{0,1},{1,0},{2,3},{3,2},{4,5},{5,4},{6,7},{7,6},{8,9},{9,8},{10,11... | collective-permute-start | bytes 6291464 | tf_op jit(solution)/shard_map/ppermute | solution.py:251
  2.4 19.8 %collective-permute-start.16 = (bf16[256,512]{1,0:T(8,128)(2,1)S(1)}, bf16[256,512]{1,0:T(8,128)(2,1)}, u32[]{:S(2)}, u32[]{:S(2)}) collective-permute-start(bf16[256,512]{1,0:T(8,128)(2,1)S(1)} %constant_dynamic-slice_fusion), channel_id=1, source_target_pairs={{4,8},{5,9},{6,10},{7,11},{8,4},{9,5},{10,6},{11,7},{20,24},{21,25... | collective-permute-start | bytes 786440 | tf_op jit(solution)/shard_map/ppermute | solution.py:251
  5.6 14.5 %collective-permute-start.11 = (bf16[256,512]{1,0:T(8,128)(2,1)S(1)}, bf16[256,512]{1,0:T(8,128)(2,1)S(1)}, u32[]{:S(2)}, u32[]{:S(2)}) collective-permute-start(bf16[256,512]{1,0:T(8,128)(2,1)S(1)} %constant_dynamic-slice_fusion), channel_id=1, source_target_pairs={{0,4},{1,5},{2,6},{3,7},{4,0},{5,1},{6,2},{7,3},{8,12},{9,13},{10,... | collective-permute-start | bytes 786440 | tf_op jit(solution)/shard_map/ppermute | solution.py:251
  5.7 1.6 %collective-permute-start.2 = (bf16[16,2048]{1,0:T(8,128)(2,1)}, bf16[16,2048]{1,0:T(8,128)(2,1)S(1)}, u32[]{:S(2)}, u32[]{:S(2)}) collective-permute-start(bf16[16,2048]{1,0:T(8,128)(2,1)} %up_own.1), channel_id=1, source_target_pairs={{0,1},{1,0},{2,3},{3,2},{4,5},{5,4},{6,7},{7,6},{8,9},{9,8},{10,11... | collective-permute-start | bytes 196616 | tf_op jit(solution)/shard_map/ppermute | solution.py:251
  6.2 67.8 %copy-start.23 = (s32[3]{0:T(128)}, s32[3]{0:T(128)S(1)}, u32[]{:S(2)}) copy-start(s32[3]{0:T(128)S(1)} %pad_add_fusion.meta) | copy-start | bytes 40
  7.3 1.2 copy-start.3
  10.0 59.2 %copy-start.28 = (s32[16,1]{0,1:T(1,128)S(1)}, s32[16,1]{0,1:T(1,128)}, u32[]{:S(2)}) copy-start(s32[16,1]{0,1:T(1,128)} %param.13) | copy-start | bytes 196
  10.0 59.2 %copy-start.32 = (s32[16]{0:T(128)S(1)}, s32[16]{0:T(128)}, u32[]{:S(2)}) copy-start(s32[16]{0:T(128)} %ranks.3) | copy-start | bytes 196
  12.4 22.4 %copy-start.34 = (bf16[144,512]{1,0:T(8,128)(2,1)}, bf16[144,512]{1,0:T(8,128)(2,1)S(1)}, u32[]{:S(2)}) copy-start(bf16[144,512]{1,0:T(8,128)(2,1)S(1)} %get-tuple-element.40) | copy-start | bytes 442372
  12.4 5.1 %collective-permute-start.3 = (bf16[144,512]{1,0:T(8,128)(2,1)S(1)}, bf16[144,512]{1,0:T(8,128)(2,1)S(1)}, u32[]{:S(2)}, u32[]{:S(2)}) collective-permute-start(bf16[144,512]{1,0:T(8,128)(2,1)S(1)} %get-tuple-element.34), channel_id=1, source_target_pairs={{0,2},{1,3},{2,0},{3,1},{4,6},{5,7},{6,4},{7,5},{8,10},{9,11},{10,... | collective-permute-start | bytes 442376 | tf_op jit(solution)/shard_map/ppermute | solution.py:251
  13.6 1.8 %collective-permute-start.1 = (bf16[128,512]{1,0:T(8,128)(2,1)}, bf16[128,512]{1,0:T(8,128)(2,1)S(1)}, u32[]{:S(2)}, u32[]{:S(2)}) collective-permute-start(bf16[128,512]{1,0:T(8,128)(2,1)} %og.1), channel_id=1, source_target_pairs={{0,1},{1,0},{2,3},{3,2},{4,5},{5,4},{6,7},{7,6},{8,9},{9,8},{10,11... | collective-permute-start | bytes 393224 | tf_op jit(solution)/shard_map/ppermute | solution.py:251
  15.4 8.7 %collective-permute-start.4 = (bf16[144,512]{1,0:T(8,128)(2,1)S(1)}, bf16[144,512]{1,0:T(8,128)(2,1)S(1)}, u32[]{:S(2)}, u32[]{:S(2)}) collective-permute-start(bf16[144,512]{1,0:T(8,128)(2,1)S(1)} %get-tuple-element.35), channel_id=1, source_target_pairs={{0,4},{1,5},{2,6},{3,7},{4,0},{5,1},{6,2},{7,3},{8,12},{9,13},{10,... | collective-permute-start | bytes 442376 | tf_op jit(solution)/shard_map/ppermute | solution.py:251
  17.4 56.6 %copy-start.4 = (bf16[144,512]{1,0:T(8,128)(2,1)}, bf16[144,512]{1,0:T(8,128)(2,1)S(1)}, u32[]{:S(2)}) copy-start(bf16[144,512]{1,0:T(8,128)(2,1)S(1)} %collective-permute-done.3.refs_1_) | copy-start | bytes 442372
  17.4 6.7 %collective-permute-start.5 = (bf16[144,512]{1,0:T(8,128)(2,1)S(1)}, bf16[144,512]{1,0:T(8,128)(2,1)S(1)}, u32[]{:S(2)}, u32[]{:S(2)}) collective-permute-start(bf16[144,512]{1,0:T(8,128)(2,1)S(1)} %get-tuple-element.36), channel_id=1, source_target_pairs={{0,6},{1,7},{2,4},{3,5},{4,2},{5,3},{6,0},{7,1},{8,14},{9,15},{10,... | collective-permute-start | bytes 442376 | tf_op jit(solution)/shard_map/ppermute | solution.py:251
  20.1 54.0 %copy-start.14 = (bf16[256,512]{1,0:T(8,128)(2,1)}, bf16[256,512]{1,0:T(8,128)(2,1)S(1)}, u32[]{:S(2)}) copy-start(bf16[256,512]{1,0:T(8,128)(2,1)S(1)} %collective-permute-done.11.refs_10_) | copy-start | bytes 786436
  20.1 14.6 %collective-permute-start.15 = (bf16[256,512]{1,0:T(8,128)(2,1)S(1)}, bf16[256,512]{1,0:T(8,128)(2,1)}, u32[]{:S(2)}, u32[]{:S(2)}) collective-permute-start(bf16[256,512]{1,0:T(8,128)(2,1)S(1)} %collective-permute-done.11.refs_10_), channel_id=1, source_target_pairs={{4,8},{5,9},{6,10},{7,11},{8,4},{9,5},{10,6},{11,7},{20,24},{21,25... | collective-permute-start | bytes 786440 | tf_op jit(solution)/shard_map/ppermute | solution.py:251
  22.2 18.2 %collective-permute-start.17 = (bf16[256,512]{1,0:T(8,128)(2,1)}, bf16[256,512]{1,0:T(8,128)(2,1)}, u32[]{:S(2)}, u32[]{:S(2)}) collective-permute-start(bf16[256,512]{1,0:T(8,128)(2,1)} %collective-permute-done.16), channel_id=1, source_target_pairs={{4,0},{5,1},{6,2},{7,3},{8,12},{9,13},{10,14},{11,15},{20,16},{21,... | collective-permute-start | bytes 786440 | tf_op jit(solution)/shard_map/ppermute | solution.py:251
  24.1 49.9 %copy-start.6 = (bf16[144,512]{1,0:T(8,128)(2,1)}, bf16[144,512]{1,0:T(8,128)(2,1)S(1)}, u32[]{:S(2)}) copy-start(bf16[144,512]{1,0:T(8,128)(2,1)S(1)} %collective-permute-done.4.refs_2_) | copy-start | bytes 442372
  24.2 12.6 %collective-permute-start.6 = (bf16[144,512]{1,0:T(8,128)(2,1)}, bf16[144,512]{1,0:T(8,128)(2,1)S(1)}, u32[]{:S(2)}, u32[]{:S(2)}) collective-permute-start(bf16[144,512]{1,0:T(8,128)(2,1)} %get-tuple-element.37), channel_id=1, source_target_pairs={{0,8},{1,9},{2,10},{3,11},{4,12},{5,13},{6,14},{7,15},{8,0},{9,1},... | collective-permute-start | bytes 442376 | tf_op jit(solution)/shard_map/ppermute | solution.py:251
  24.2 49.9 %copy-start.8 = (bf16[144,512]{1,0:T(8,128)(2,1)}, bf16[144,512]{1,0:T(8,128)(2,1)S(1)}, u32[]{:S(2)}) copy-start(bf16[144,512]{1,0:T(8,128)(2,1)S(1)} %collective-permute-done.5.refs_3_) | copy-start | bytes 442372
  24.2 14.8 %collective-permute-start.7 = (bf16[144,512]{1,0:T(8,128)(2,1)}, bf16[144,512]{1,0:T(8,128)(2,1)S(1)}, u32[]{:S(2)}, u32[]{:S(2)}) collective-permute-start(bf16[144,512]{1,0:T(8,128)(2,1)} %get-tuple-element.38), channel_id=1, source_target_pairs={{0,10},{1,11},{2,8},{3,9},{4,14},{5,15},{6,12},{7,13},{8,2},{9,3},... | collective-permute-start | bytes 442376 | tf_op jit(solution)/shard_map/ppermute | solution.py:251
  34.7 13.4 %collective-permute-start.21 = (bf16[256,512]{1,0:T(8,128)(2,1)}, bf16[256,512]{1,0:T(8,128)(2,1)}, u32[]{:S(2)}, u32[]{:S(2)}) collective-permute-start(bf16[256,512]{1,0:T(8,128)(2,1)} %collective-permute-done.15), channel_id=1, source_target_pairs={{4,0},{5,1},{6,2},{7,3},{8,12},{9,13},{10,14},{11,15},{20,16},{21,... | collective-permute-start | bytes 786440 | tf_op jit(solution)/shard_map/ppermute | solution.py:251
  36.7 37.3 %copy-start.10 = (bf16[144,512]{1,0:T(8,128)(2,1)}, bf16[144,512]{1,0:T(8,128)(2,1)S(1)}, u32[]{:S(2)}) copy-start(bf16[144,512]{1,0:T(8,128)(2,1)S(1)} %collective-permute-done.6.refs_4_) | copy-start | bytes 442372
  36.7 17.1 %collective-permute-start.10 = (bf16[512,512]{1,0:T(8,128)(2,1)}, bf16[512,512]{1,0:T(8,128)(2,1)S(1)}, u32[]{:S(2)}, u32[]{:S(2)}) collective-permute-start(bf16[512,512]{1,0:T(8,128)(2,1)} %refs_8_.1), channel_id=1, source_target_pairs={{0,2},{1,3},{2,0},{3,1},{4,6},{5,7},{6,4},{7,5},{8,10},{9,11},{10,... | collective-permute-start | bytes 1572872 | tf_op jit(solution)/shard_map/ppermute | solution.py:251
  39.0 35.1 %copy-start.12 = (bf16[144,512]{1,0:T(8,128)(2,1)}, bf16[144,512]{1,0:T(8,128)(2,1)S(1)}, u32[]{:S(2)}) copy-start(bf16[144,512]{1,0:T(8,128)(2,1)S(1)} %collective-permute-done.7.refs_5_) | copy-start | bytes 442372
  39.0 5.2 %collective-permute-start.8 = (bf16[144,512]{1,0:T(8,128)(2,1)}, bf16[144,512]{1,0:T(8,128)(2,1)S(1)}, u32[]{:S(2)}, u32[]{:S(2)}) collective-permute-start(bf16[144,512]{1,0:T(8,128)(2,1)} %copy-done.35), channel_id=1, source_target_pairs={{0,12},{1,13},{2,14},{3,15},{4,8},{5,9},{6,10},{7,11},{8,4},{9,5},... | collective-permute-start | bytes 442376 | tf_op jit(solution)/shard_map/ppermute | solution.py:251
  40.4 12.8 %collective-permute-start.13 = (bf16[256,512]{1,0:T(8,128)(2,1)S(1)}, bf16[256,512]{1,0:T(8,128)(2,1)S(1)}, u32[]{:S(2)}, u32[]{:S(2)}) collective-permute-start(bf16[256,512]{1,0:T(8,128)(2,1)S(1)} %collective-permute-done.11.refs_10_), channel_id=1, source_target_pairs={{0,2},{1,3},{2,0},{3,1},{4,6},{5,7},{6,4},{7,5},{8,10},{9,11},{10,... | collective-permute-start | bytes 786440 | tf_op jit(solution)/shard_map/ppermute | solution.py:251
  44.3 7.8 %collective-permute-start.9 = (bf16[144,512]{1,0:T(8,128)(2,1)}, bf16[144,512]{1,0:T(8,128)(2,1)S(1)}, u32[]{:S(2)}, u32[]{:S(2)}) collective-permute-start(bf16[144,512]{1,0:T(8,128)(2,1)} %copy-done.34), channel_id=1, source_target_pairs={{0,14},{1,15},{2,12},{3,13},{4,10},{5,11},{6,8},{7,9},{8,6},{9,7},... | collective-permute-start | bytes 442376 | tf_op jit(solution)/shard_map/ppermute | solution.py:251
  48.1 5.5 %collective-permute-start.12 = (bf16[256,512]{1,0:T(8,128)(2,1)S(1)}, bf16[256,512]{1,0:T(8,128)(2,1)S(1)}, u32[]{:S(2)}, u32[]{:S(2)}) collective-permute-start(bf16[256,512]{1,0:T(8,128)(2,1)S(1)} %collective-permute-done.11.refs_10_), channel_id=1, source_target_pairs={{0,16},{1,17},{2,18},{3,19},{4,20},{5,21},{6,22},{7,23},{8,24},{9,... | collective-permute-start | bytes 786440 | tf_op jit(solution)/shard_map/ppermute | solution.py:251
  52.1 10.0 %collective-permute-start.19 = (bf16[256,512]{1,0:T(8,128)(2,1)S(1)}, bf16[256,512]{1,0:T(8,128)(2,1)S(1)}, u32[]{:S(2)}, u32[]{:S(2)}) collective-permute-start(bf16[256,512]{1,0:T(8,128)(2,1)S(1)} %broadcast_select_fusion.1.refs_14_), channel_id=1, source_target_pairs={{0,2},{1,3},{2,0},{3,1},{4,6},{5,7},{6,4},{7,5},{8,10},{9,11},{10,... | collective-permute-start | bytes 786440 | tf_op jit(solution)/shard_map/ppermute | solution.py:251
  53.2 14.5 %collective-permute-start.23 = (bf16[256,512]{1,0:T(8,128)(2,1)S(1)}, bf16[256,512]{1,0:T(8,128)(2,1)S(1)}, u32[]{:S(2)}, u32[]{:S(2)}) collective-permute-start(bf16[256,512]{1,0:T(8,128)(2,1)S(1)} %broadcast_select_fusion.refs_18_), channel_id=1, source_target_pairs={{0,2},{1,3},{2,0},{3,1},{4,6},{5,7},{6,4},{7,5},{8,10},{9,11},{10,... | collective-permute-start | bytes 786440 | tf_op jit(solution)/shard_map/ppermute | solution.py:251
  53.6 21.1 %collective-permute-start.18 = (bf16[256,512]{1,0:T(8,128)(2,1)S(1)}, bf16[256,512]{1,0:T(8,128)(2,1)S(1)}, u32[]{:S(2)}, u32[]{:S(2)}) collective-permute-start(bf16[256,512]{1,0:T(8,128)(2,1)S(1)} %broadcast_select_fusion.1.refs_14_), channel_id=1, source_target_pairs={{0,16},{1,17},{2,18},{3,19},{4,20},{5,21},{6,22},{7,23},{8,24},{9,... | collective-permute-start | bytes 786440 | tf_op jit(solution)/shard_map/ppermute | solution.py:251
  53.9 20.9 %collective-permute-start.14 = (bf16[256,512]{1,0:T(8,128)(2,1)S(1)}, bf16[256,512]{1,0:T(8,128)(2,1)S(1)}, u32[]{:S(2)}, u32[]{:S(2)}) collective-permute-start(bf16[256,512]{1,0:T(8,128)(2,1)S(1)} %collective-permute-done.13.refs_12_), channel_id=1, source_target_pairs={{0,16},{1,17},{2,18},{3,19},{4,20},{5,21},{6,22},{7,23},{8,24},{9,... | collective-permute-start | bytes 786440 | tf_op jit(solution)/shard_map/ppermute | solution.py:251
  62.1 14.0 %collective-permute-start.22 = (bf16[256,512]{1,0:T(8,128)(2,1)S(1)}, bf16[256,512]{1,0:T(8,128)(2,1)S(1)}, u32[]{:S(2)}, u32[]{:S(2)}) collective-permute-start(bf16[256,512]{1,0:T(8,128)(2,1)S(1)} %broadcast_select_fusion.refs_18_), channel_id=1, source_target_pairs={{0,16},{1,17},{2,18},{3,19},{4,20},{5,21},{6,22},{7,23},{8,24},{9,... | collective-permute-start | bytes 786440 | tf_op jit(solution)/shard_map/ppermute | solution.py:251
  67.7 8.4 %collective-permute-start.20 = (bf16[256,512]{1,0:T(8,128)(2,1)S(1)}, bf16[256,512]{1,0:T(8,128)(2,1)S(1)}, u32[]{:S(2)}, u32[]{:S(2)}) collective-permute-start(bf16[256,512]{1,0:T(8,128)(2,1)S(1)} %collective-permute-done.19.refs_16_), channel_id=1, source_target_pairs={{0,16},{1,17},{2,18},{3,19},{4,20},{5,21},{6,22},{7,23},{8,24},{9,... | collective-permute-start | bytes 786440 | tf_op jit(solution)/shard_map/ppermute | solution.py:251
  67.9 13.7 %collective-permute-start.24 = (bf16[256,512]{1,0:T(8,128)(2,1)S(1)}, bf16[256,512]{1,0:T(8,128)(2,1)S(1)}, u32[]{:S(2)}, u32[]{:S(2)}) collective-permute-start(bf16[256,512]{1,0:T(8,128)(2,1)S(1)} %collective-permute-done.23.refs_20_), channel_id=1, source_target_pairs={{0,16},{1,17},{2,18},{3,19},{4,20},{5,21},{6,22},{7,23},{8,24},{9,... | collective-permute-start | bytes 786440 | tf_op jit(solution)/shard_map/ppermute | solution.py:251
  69.2 12.5 %copy-start.2 = (bf16[512,512]{1,0:T(8,128)(2,1)S(1)}, bf16[512,512]{1,0:T(8,128)(2,1)}, u32[]{:S(2)}) copy-start(bf16[512,512]{1,0:T(8,128)(2,1)} %refs_8_.1) | copy-start | bytes 1572868
  81.7 0.9 copy-start.5
  82.6 0.9 copy-start.7
  83.5 0.9 copy-start.9
  84.4 0.9 copy-start.11
  85.3 0.9 copy-start.13
  86.2 0.9 copy-start.15
  87.8 27.5 %copy-start.29 = (s32[16,1]{0,1:T(1,128)S(1)}, s32[16,1]{0,1:T(1,128)}, u32[]{:S(2)}) copy-start(s32[16,1]{0,1:T(1,128)} %param.13) | copy-start | bytes 196
  87.8 27.5 %copy-start.33 = (s32[16]{0:T(128)S(1)}, s32[16]{0:T(128)}, u32[]{:S(2)}) copy-start(s32[16]{0:T(128)} %ranks.3) | copy-start | bytes 196
  93.5 23.7 %copy-start.16 = (f32[128,512]{1,0:T(8,128)}, f32[128,512]{1,0:T(8,128)S(1)}, u32[]{:S(2)}) copy-start(f32[128,512]{1,0:T(8,128)S(1)} %get-tuple-element.43.mine) | copy-start | bytes 786436
  93.5 45.2 %copy-start.31 = (s32[16,1]{0,1:T(1,128)S(1)}, s32[16,1]{0,1:T(1,128)}, u32[]{:S(2)}) copy-start(s32[16,1]{0,1:T(1,128)} %param.13) | copy-start | bytes 196
  93.5 46.6 %copy-start.26 = (s32[3]{0:T(128)S(1)}, s32[3]{0:T(128)}, u32[]{:S(2)}) copy-start(s32[3]{0:T(128)} %copy-done.23) | copy-start | bytes 40
  93.5 46.6 %collective-permute-start.27 = (bf16[128,4096]{1,0:T(8,128)(2,1)}, bf16[128,4096]{1,0:T(8,128)(2,1)S(1)}, u32[]{:S(2)}, u32[]{:S(2)}) collective-permute-start(bf16[128,4096]{1,0:T(8,128)(2,1)} %get-tuple-element.50), channel_id=1, source_target_pairs={{0,1},{1,0},{2,3},{3,2},{4,5},{5,4},{6,7},{7,6},{8,9},{9,8},{10,11... | collective-permute-start | bytes 3145736 | tf_op jit(solution)/shard_map/ppermute | solution.py:251
  99.5 8.2 %collective-permute-start.28 = (bf16[128,512]{1,0:T(8,128)(2,1)S(1)}, bf16[128,512]{1,0:T(8,128)(2,1)S(1)}, u32[]{:S(2)}, u32[]{:S(2)}) collective-permute-start(bf16[128,512]{1,0:T(8,128)(2,1)S(1)} %get-tuple-element.54), channel_id=1, source_target_pairs={{0,2},{1,3},{2,0},{3,1},{4,6},{5,7},{6,4},{7,5},{8,10},{9,11},{10,... | collective-permute-start | bytes 393224 | tf_op jit(solution)/shard_map/ppermute | solution.py:251
  100.1 5.0 %collective-permute-start.26 = (f32[128,64]{1,0:T(8,128)S(1)}, f32[128,64]{1,0:T(8,128)S(1)}, u32[]{:S(2)}, u32[]{:S(2)}) collective-permute-start(f32[128,64]{1,0:T(8,128)S(1)} %get-tuple-element.46), channel_id=1, source_target_pairs={{0,1},{1,0},{2,3},{3,2},{4,5},{5,4},{6,7},{7,6},{8,9},{9,8},{10,11... | collective-permute-start | bytes 98312 | tf_op jit(solution)/shard_map/ppermute | solution.py:251
  100.5 8.4 %collective-permute-start.29 = (bf16[128,512]{1,0:T(8,128)(2,1)S(1)}, bf16[128,512]{1,0:T(8,128)(2,1)S(1)}, u32[]{:S(2)}, u32[]{:S(2)}) collective-permute-start(bf16[128,512]{1,0:T(8,128)(2,1)S(1)} %get-tuple-element.55), channel_id=1, source_target_pairs={{0,4},{1,5},{2,6},{3,7},{4,0},{5,1},{6,2},{7,3},{8,12},{9,13},{10,... | collective-permute-start | bytes 393224 | tf_op jit(solution)/shard_map/ppermute | solution.py:251
  105.1 8.3 %collective-permute-start.30 = (bf16[128,512]{1,0:T(8,128)(2,1)S(1)}, bf16[128,512]{1,0:T(8,128)(2,1)S(1)}, u32[]{:S(2)}, u32[]{:S(2)}) collective-permute-start(bf16[128,512]{1,0:T(8,128)(2,1)S(1)} %get-tuple-element.56), channel_id=1, source_target_pairs={{0,6},{1,7},{2,4},{3,5},{4,2},{5,3},{6,0},{7,1},{8,14},{9,15},{10,... | collective-permute-start | bytes 393224 | tf_op jit(solution)/shard_map/ppermute | solution.py:251
  105.1 9.2 %collective-permute-start.31 = (bf16[128,512]{1,0:T(8,128)(2,1)S(1)}, bf16[128,512]{1,0:T(8,128)(2,1)S(1)}, u32[]{:S(2)}, u32[]{:S(2)}) collective-permute-start(bf16[128,512]{1,0:T(8,128)(2,1)S(1)} %get-tuple-element.57), channel_id=1, source_target_pairs={{0,8},{1,9},{2,10},{3,11},{4,12},{5,13},{6,14},{7,15},{8,0},{9,1},... | collective-permute-start | bytes 393224 | tf_op jit(solution)/shard_map/ppermute | solution.py:251
  107.6 32.5 %collective-permute-start.25 = (f32[128,512]{1,0:T(8,128)}, f32[128,512]{1,0:T(8,128)S(1)}, u32[]{:S(2)}, u32[]{:S(2)}) collective-permute-start(f32[128,512]{1,0:T(8,128)} %get-tuple-element.44), channel_id=1, source_target_pairs={{0,1},{1,0},{2,3},{3,2},{4,5},{5,4},{6,7},{7,6},{8,9},{9,8},{10,11... | collective-permute-start | bytes 786440 | tf_op jit(solution)/shard_map/ppermute | solution.py:251
  108.9 18.3 %collective-permute-start.32 = (bf16[128,512]{1,0:T(8,128)(2,1)}, bf16[128,512]{1,0:T(8,128)(2,1)}, u32[]{:S(2)}, u32[]{:S(2)}) collective-permute-start(bf16[128,512]{1,0:T(8,128)(2,1)} %get-tuple-element.58), channel_id=1, source_target_pairs={{0,10},{1,11},{2,8},{3,9},{4,14},{5,15},{6,12},{7,13},{8,2},{9,3},... | collective-permute-start | bytes 393224 | tf_op jit(solution)/shard_map/ppermute | solution.py:251
  113.4 15.5 %collective-permute-start.33 = (bf16[128,512]{1,0:T(8,128)(2,1)}, bf16[128,512]{1,0:T(8,128)(2,1)}, u32[]{:S(2)}, u32[]{:S(2)}) collective-permute-start(bf16[128,512]{1,0:T(8,128)(2,1)} %get-tuple-element.59), channel_id=1, source_target_pairs={{0,12},{1,13},{2,14},{3,15},{4,8},{5,9},{6,10},{7,11},{8,4},{9,5},... | collective-permute-start | bytes 393224 | tf_op jit(solution)/shard_map/ppermute | solution.py:251
  114.3 2.9 %copy-start.20 = (bf16[128,512]{1,0:T(8,128)(2,1)}, bf16[128,512]{1,0:T(8,128)(2,1)S(1)}, u32[]{:S(2)}) copy-start(bf16[128,512]{1,0:T(8,128)(2,1)S(1)} %collective-permute-done.31.refs_4_) | copy-start | bytes 393220
  114.3 19.2 %collective-permute-start.34 = (bf16[128,512]{1,0:T(8,128)(2,1)}, bf16[128,512]{1,0:T(8,128)(2,1)}, u32[]{:S(2)}, u32[]{:S(2)}) collective-permute-start(bf16[128,512]{1,0:T(8,128)(2,1)} %get-tuple-element.60), channel_id=1, source_target_pairs={{0,14},{1,15},{2,12},{3,13},{4,10},{5,11},{6,8},{7,9},{8,6},{9,7},... | collective-permute-start | bytes 393224 | tf_op jit(solution)/shard_map/ppermute | solution.py:251
  117.2 22.9 %copy-start.17 = (f32[128,512]{1,0:T(8,128)S(1)}, f32[128,512]{1,0:T(8,128)}, u32[]{:S(2)}) copy-start(f32[128,512]{1,0:T(8,128)} %copy-done.16) | copy-start | bytes 786436
  117.2 21.5 %all-to-all-start = ((bf16[16,16,128]{2,1,0:T(8,128)(2,1)}), bf16[16,16,128]{2,1,0:T(8,128)(2,1)S(1)}, u32[]{:S(2)}, u32[]{:S(2)}) async-start(bf16[16,16,128]{2,1,0:T(8,128)(2,1)} %get-tuple-element.61), calls=%async_computation | async-start | bytes 131072 | tf_op jit(solution)/shard_map/all_to_all | solution.py:295
  133.5 0.9 copy-start.19
  (8 other events, 5.6 us)

commit v3 on v2

v3 whole, which is shorter than its diff:
```python
import functools

import jax
import jax.numpy as jnp
from jax import lax
from jax.experimental import pallas as pl
from jax.experimental.pallas import tpu as pltpu
from jax.sharding import PartitionSpec as P

RANK_TILE = 16
AXES = ("groups", "dp")
F32 = jnp.float32
BF16 = jnp.bfloat16
VMEM = pl.BlockSpec(memory_space=pltpu.VMEM)
SMEM = pl.BlockSpec(memory_space=pltpu.SMEM)


def dot(a, b, ca, cb):
    return lax.dot_general(a, b, (((ca,), (cb,)), ((), ())), preferred_element_type=F32)


def call(kernel, outs, scalars, arrays, flops=0):
    size = sum(x.size * x.dtype.itemsize for x in arrays)
    size += sum(x.size * x.dtype.itemsize for x in outs)
    return pl.pallas_call(
        kernel,
        out_shape=outs,
        in_specs=[SMEM] * len(scalars) + [VMEM] * len(arrays),
        out_specs=[VMEM] * len(outs),
        compiler_params=pltpu.CompilerParams(vmem_limit_bytes=60 * 1024 * 1024),
        cost_estimate=pl.CostEstimate(flops=flops, bytes_accessed=size, transcendentals=0),
    )(*scalars, *arrays)


def shape(dims, dtype=BF16):
    return jax.ShapeDtypeStruct(dims, dtype)


def iota(dims, axis):
    return lax.broadcasted_iota(jnp.int32, dims, axis)


def factor_of(ids, ranks, tile, width):
    count = ranks[ids[tile]]
    scale = 2.0 / jnp.full((1, width), count, jnp.int32).astype(F32)
    return jnp.where(iota((1, width), 1) < count * RANK_TILE, scale, 0.0)


def pack_kernel(meta, ids, down, up_own, up_other, blocks):
    adapters, rank, width = down.shape
    chips = blocks.shape[0]
    c = meta[1]
    rows = chips * 16
    q = iota((rows, adapters), 0)
    chosen = jnp.zeros((rows, adapters), jnp.int32)
    for chip in range(chips):
        for slot in range(2):
            adapter = ids[2 * chip + jnp.bitwise_xor(c, slot)]
            blocks[chip, rank * slot : rank * (slot + 1), :] = down[adapter]
            chosen = jnp.where(q // 8 == 2 * chip + slot, adapter, chosen)
    match = chosen == iota((rows, adapters), 1)
    packed = jnp.zeros((rows, width), F32)
    for side, up in enumerate((up_own, up_other)):
        for r in range(4):
            pick = (match & (q % 8 == 4 * side + r)).astype(F32).astype(BF16)
            packed = packed + dot(pick, up[:, width * r : width * (r + 1)], 1, 0)
    packed = packed.astype(BF16)
    for chip in range(chips):
        blocks[chip, 2 * rank : 2 * rank + 16, :] = packed[16 * chip : 16 * (chip + 1), :]


def lane_masks(out_width, width, rank):
    per_row = width // rank
    lane_ok = iota((out_width, width), 1) // rank == iota((out_width, width), 0) % per_row
    fold = (iota((width, rank), 0) % rank == iota((width, rank), 1)).astype(F32).astype(BF16)
    return lane_ok, fold


def rank_kernel(
    meta, ids, ranks, tok_own, tok_sib, og_own, og_sib, blocks, grads, low, back_own, back_sib, up_out
):
    chips, _, width = blocks.shape
    rows = tok_own.shape[0]
    out_width = og_own.shape[1]
    rank = back_own.shape[1]
    k, c = meta[0], meta[1]
    heads = out_width // (2 * chips)
    per_row = width // rank
    packed = jnp.concatenate([blocks[i, 2 * rank : 2 * rank + 16, :] for i in range(chips)], axis=0)
    q = iota((out_width, chips * 16), 1)
    o = iota((out_width, chips * 16), 0)
    device = 2 * (q // 16) + jnp.bitwise_xor(c, (q // 4) % 2)
    place = o // per_row == device * (heads // per_row) + q % 4
    lane_ok, fold = lane_masks(out_width, width, rank)
    for slot, (tok, og, back) in enumerate(
        ((tok_own, og_own, back_own), (tok_sib, og_sib, back_sib))
    ):
        pick = (place & ((q // 8) % 2 == slot)).astype(F32).astype(BF16)
        spread = jnp.where(lane_ok, dot(pick, packed, 1, 0), 0.0).astype(BF16)
        up = dot(spread, fold, 1, 0).astype(BF16)
        if slot == 0:
            up_out[...] = up
        factor = factor_of(ids, ranks, 2 * k + jnp.bitwise_xor(c, slot), rank)
        backward = (dot(og[...], up, 1, 0) * factor).astype(BF16)
        back[...] = backward
        turned = backward.T
        total = jnp.zeros((rows, rank), F32)
        half = slice(rank * slot, rank * (slot + 1))
        for i in range(chips):
            start = pl.multiple_of((2 * i + c) * width, width)
            part = tok[:, pl.ds(start, width)]
            grads[i, half, :] = dot(turned, part, 1, 0).astype(BF16)
            total = total + dot(part, blocks[i, half, :], 1, 1)
        low[rows * slot : rows * (slot + 1), :] = total


def hidden_kernel(chips, meta, ids, ranks, low, other, og_own, og_sib, up, out_low, *terms):
    rows, out_width = og_own.shape
    rank = up.shape[1]
    width = terms[0].shape[1]
    k, c = meta[0], meta[1]
    heads = out_width // (2 * chips)
    per_row = width // rank
    q = iota((chips * 8, out_width), 0)
    o = iota((chips * 8, out_width), 1)
    device = 2 * jnp.bitwise_xor(k, q // 8) + c
    place = o // per_row == device * (heads // per_row) + q % 4
    lane_ok, fold = lane_masks(out_width, width, rank)
    packed = jnp.zeros((chips * 8, width), F32)
    for slot, og in enumerate((og_own, og_sib)):
        factor = factor_of(ids, ranks, 2 * k + jnp.bitwise_xor(c, slot), rank)
        total = low[rows * slot : rows * (slot + 1), :] + other[rows * (1 - slot) : rows * (2 - slot), :]
        hidden = (total * factor).astype(BF16)
        if slot == 0:
            out_low[...] = dot(hidden, up[...], 1, 1)
        term = dot(og[...], hidden, 0, 0).astype(BF16)
        spread = jnp.where(lane_ok, dot(term, fold, 1, 1), 0.0).astype(BF16)
        pick = (place & ((q // 4) % 2 == slot)).astype(F32).astype(BF16)
        packed = packed + dot(pick, spread, 1, 0)
    for j in range(chips):
        terms[j][...] = packed[8 * j : 8 * (j + 1), :].astype(BF16)


def base_kernel(plan, meta, tok_own, tok_sib, og_own, og_sib, back_own, back_sib, blocks, *refs):
    pieces = refs[: len(refs) - 4]
    for_own, for_sib, grad_own, grad_sib = refs[len(refs) - 4 :]
    width = blocks.shape[2]
    rank = back_own.shape[1]
    rows = tok_own.shape[0]
    k, c, g = meta[0], meta[1], meta[2]
    og = jnp.concatenate([og_own[...], og_sib[...]], axis=0)
    total = jnp.zeros((2 * rows, og.shape[1]), F32)
    for index, j, count, side in plan:
        piece = pieces[index]
        chip = jnp.bitwise_xor(k, j)
        shift = 0 if side is None else jnp.bitwise_xor(g, side) * count
        if piece.shape[0] > count:
            weight = piece[pl.ds(pl.multiple_of(chip * count, count), count), :]
        else:
            weight = piece[...]
        start = pl.multiple_of((2 * chip + c) * width + shift, 128)
        tok = jnp.concatenate(
            [tok_own[:, pl.ds(start, count)], tok_sib[:, pl.ds(start, count)]], axis=0
        )
        total = total + dot(tok, weight, 1, 0)
        grad = dot(og, weight, 1, 1)
        inner = pl.ds(pl.multiple_of(shift, 128), count)
        low_own = dot(back_own[...], blocks[chip, 0:rank, inner], 1, 0).astype(BF16)
        low_sib = dot(back_sib[...], blocks[chip, rank : 2 * rank, inner], 1, 0).astype(BF16)
        to = pl.ds(pl.multiple_of(chip * width + shift, 128), count)
        grad_own[:, to] = (grad[:rows] + low_own.astype(F32)).astype(BF16)
        grad_sib[:, to] = (grad[rows:] + low_sib.astype(F32)).astype(BF16)
    for_own[...] = total[:rows]
    for_sib[...] = total[rows:]


def join_kernel(chips, meta, mine, other, out_low, grad_mine, grad_other, result, grad_in):
    c = meta[1]
    result[...] = (mine[...] + other[...] + out_low[...]).astype(BF16)
    width = grad_mine.shape[1] // chips
    for chip in range(chips):
        cols = slice(width * chip, width * (chip + 1))
        own = pl.multiple_of((2 * chip + c) * width, width)
        sib = pl.multiple_of((2 * chip + 1 - c) * width, width)
        grad_in[:, pl.ds(own, width)] = grad_mine[:, cols]
        grad_in[:, pl.ds(sib, width)] = grad_other[:, cols]


def down_kernel(meta, ids, back, out):
    rank = out.shape[1]
    c = meta[1]
    for chip in range(back.shape[0]):
        for slot in range(2):
            adapter = ids[2 * chip + jnp.bitwise_xor(c, slot)]
            out[adapter] = back[chip, rank * slot : rank * (slot + 1), :]


def up_kernel(meta, ids, *refs):
    out, terms = refs[-1], refs[:-1]
    width = terms[0].shape[1]
    k, c = meta[0], meta[1]
    flat = jnp.concatenate([t[...] for t in terms], axis=0)
    q = iota((out.shape[0], flat.shape[0]), 1)
    chosen = jnp.zeros(q.shape, jnp.int32)
    for j in range(len(terms)):
        for slot in range(2):
            adapter = ids[2 * jnp.bitwise_xor(k, j) + jnp.bitwise_xor(c, slot)]
            chosen = jnp.where(q // 4 == 2 * j + slot, adapter, chosen)
    match = chosen == iota(q.shape, 0)
    for r in range(4):
        pick = (match & (q % 4 == r)).astype(F32).astype(BF16)
        out[:, width * r : width * (r + 1)] = dot(pick, flat, 1, 0).astype(BF16)


def pairs(groups, size, to):
    out = []
    for g in range(groups):
        for d in range(size):
            target = to(g, d)
            if target is not None:
                out.append((g * size + d, target[0] * size + target[1]))
    return out


def gather_weight(weight, groups, size, send):
    chips = size // 2
    rows = weight.shape[0]
    if groups != 2 or chips != 8:
        lists = [[2 * chip + core for chip in range(chips)] for core in range(2)]
        full = lax.all_gather(weight, "dp", axis=0, tiled=True, axis_index_groups=lists)
        return [full], [(0, j, rows, None) for j in range(chips)]
    half = rows // 2
    place = lax.axis_index("dp")
    z = place // 4
    middle = (z == 1) | (z == 2)
    mine = lax.dynamic_slice_in_dim(weight, lax.axis_index("groups") * half, half)
    swap_x = lambda g, d: (1 - g, d)
    swap_y = lambda g, d: (g, d ^ 2)
    swap_near = lambda g, d: (g, d ^ 4)
    swap_mid = lambda g, d: (g, d ^ 12) if d // 4 in (1, 2) else None
    outward = lambda g, d: (g, d ^ 4) if d // 4 in (1, 2) else None
    near = send(mine, swap_near)
    cross = send(mine, swap_mid)
    own_y = send(weight, swap_y)
    cross_near = send(near, swap_mid)
    edge = send(cross, outward)
    edge_near = send(cross_near, outward)
    by_slot = (
        (2, near),
        (4, jnp.where(middle, cross_near, edge)),
        (6, jnp.where(middle, cross, edge_near)),
    )
    arrays = [weight, own_y]
    plan = [(0, 0, rows, None), (1, 1, rows, None)]
    for j, held in by_slot:
        over_y = send(held, swap_y)
        first = len(arrays)
        arrays += [held, send(held, swap_x), over_y, send(over_y, swap_x)]
        plan += [(first + i, j + i // 2, half, i % 2) for i in range(4)]
    return arrays, plan


def body(groups, size, tokens, out_grad, base_weight, adapter_down, adapter_up, rank_tiles, tile_adapter):
    chips = size // 2
    rows, model_width = tokens.shape
    out_width = out_grad.shape[1]
    adapters, rank, width = adapter_down.shape
    ids = tile_adapter[:, 0]
    place = lax.axis_index("dp")
    meta = jnp.stack([place // 2, place % 2, lax.axis_index("groups")]).astype(jnp.int32)

    def send(x, to):
        return lax.ppermute(x, AXES, pairs(groups, size, to))

    def sibling(x):
        return send(x, lambda g, d: (g, d ^ 1))

    same_core = [[2 * chip + core for chip in range(chips)] for core in range(2)]

    def exchange(blocks):
        return lax.all_to_all(
            blocks, "dp", split_axis=0, concat_axis=0, tiled=True, axis_index_groups=same_core
        )

    up_sib = sibling(adapter_up)
    tok_sib = sibling(tokens)
    og_sib = sibling(out_grad)
    (packed,) = call(
        pack_kernel,
        [shape((chips, 2 * rank + 16, width))],
        (meta, ids),
        (adapter_down, adapter_up, up_sib),
    )
    blocks = exchange(packed)
    weights, plan = gather_weight(base_weight, groups, size, send)

    grads, low, back_own, back_sib, up_mine = call(
        rank_kernel,
        [
            shape((chips, 2 * rank, width)),
            shape((2 * rows, rank), F32),
            shape((rows, rank)),
            shape((rows, rank)),
            shape((out_width, rank)),
        ],
        (meta, ids, rank_tiles),
        (tokens, tok_sib, out_grad, og_sib, blocks),
        flops=4 * rows * model_width * rank,
    )
    grads_back = exchange(grads)
    out_low, *terms = call(
        functools.partial(hidden_kernel, chips),
        [shape((rows, out_width), F32)] + [shape((8, width))] * chips,
        (meta, ids, rank_tiles),
        (low, sibling(low), out_grad, og_sib, up_mine),
        flops=4 * rows * out_width * rank,
    )
    terms_back = terms[:1] + [
        send(terms[j], lambda g, d: (g, d ^ (2 * j))) for j in range(1, chips)
    ]
    (up_grad,) = call(up_kernel, [shape(adapter_up.shape)], (meta, ids), tuple(terms_back))

    for_own, for_sib, grad_own, grad_sib = call(
        functools.partial(base_kernel, plan),
        [shape((rows, out_width), F32)] * 2 + [shape((rows, model_width // 2))] * 2,
        (meta,),
        (tokens, tok_sib, out_grad, og_sib, back_own, back_sib, blocks, *weights),
        flops=4 * rows * model_width * out_width,
    )
    for_other, grad_other = sibling(for_sib), sibling(grad_sib)
    result, grad_in = call(
        functools.partial(join_kernel, chips),
        [shape((rows, out_width)), shape((rows, model_width))],
        (meta,),
        (for_own, for_other, out_low, grad_own, grad_other),
    )
    (down_grad,) = call(
        down_kernel,
        [shape(adapter_down.shape)],
        (meta, ids),
        (grads_back,),
    )
    return result, grad_in, down_grad, up_grad


def solution(mesh):
    return jax.shard_map(
        functools.partial(body, mesh.shape["groups"], mesh.shape["dp"]),
        mesh=mesh,
        in_specs=(
            P(("groups", "dp"), None),
            P(("groups", "dp"), None),
            P("dp", None),
            P(None, None, "dp"),
            P(None, "dp"),
            P(),
            P("groups", None),
        ),
        out_specs=(
            P(("groups", "dp"), None),
            P(("groups", "dp"), None),
            P("groups", None, "dp"),
            P("groups", "dp"),
        ),
        check_vma=False,
    )
```

time: 143 us -> 151 us (1.056)
  the two profiles are of different devices: /device:TPU:11 before, /device:TPU:0 now
where the time goes in v3:
time: 151 us; the launch traced here: 150 us
  waiting for transfers between devices  64.4 us (43%)
  starting transfers between devices  47.3 us (31%)
  Pallas kernels  27 us (18%)
  local copies, waits for them, and re-layouts  7.48 us (5%)
  other arithmetic  3.35 us (2%)
    ppermute x28, waiting for transfers between devices, send(): return lax.ppermute(x, AXES, pairs(groups, size, to))  64.4 us
    ppermute x28, starting transfers between devices, send(): return lax.ppermute(x, AXES, pairs(groups, size, to))  33.4 us
    pallas_call x7, Pallas kernels, call(): pl.pallas_call(kernel, out_shape=outs, in_specs=[SMEM] * len(scalars) + [...  27 us
    all_to_all x2, starting transfers between devices, exchange(): lax.all_to_all(blocks, 'dp', split_axis=0, concat_axis=0, tiled=True, axi...  13.9 us
    unnamed x48, local copies, waits for them, and re-layouts  6.51 us
  transfers between devices with their start and end apart: 30, of which 11 were waited for; matrix products, arithmetic and copies ran while one was open for 3% of the time, Pallas kernels for 16%

profile of v3, /device:TPU:0, one launch (start us, length us, event | category | flops | bytes accessed | tf_op | source)
XLA Modules:
  0.0 150.3 jit_solution(11524197191970685212)
XLA Ops:
  0.6 0.5 collective-permute-start.2
  1.1 0.1 collective-permute-start
  1.2 0.7 pad_add_fusion.meta
  1.9 0.4 collective-permute-done.2.up_other
  2.3 0.6 copy-done.16
  2.9 2.8 %shard_map.102 = bf16[8,144,512]{2,1,0:T(8,128)(2,1)} custom-call(s32[3]{0:T(128)} %pad_add_fusion.meta, s32[16]{0:T(128)} %bitcast.4, bf16[16,64,512]{2,1,0:T(8,128)(2,1)} %down.1, bf16[16,2048]{1,0:T(8,128)(2,1)} %up_own.1, bf16[16,2048]{1,0:T(8,128)(2,1)} %copy-done.16), custom_call_target="tpu_custom_call" | custom-call | bytes 2359296 | tf_op jit(solution)/shard_map/pallas_call | solution.py:25
  5.7 7.2 %all-to-all-start = ((bf16[8,144,512]{2,1,0:T(8,128)(2,1)}), bf16[8,144,512]{2,1,0:T(8,128)(2,1)S(1)}, u32[]{:S(2)}, u32[]{:S(2)}) async-start(bf16[8,144,512]{2,1,0:T(8,128)(2,1)} %shard_map.102), calls=%async_computation | async-start | bytes 2359296 | tf_op jit(solution)/shard_map/all_to_all | solution.py:281
  12.9 1.0 constant_dynamic-slice_fusion
  13.9 1.4 collective-permute-start.9
  15.2 4.1 %collective-permute-start.4 = (bf16[256,512]{1,0:T(8,128)(2,1)S(1)}, bf16[256,512]{1,0:T(8,128)(2,1)}, u32[]{:S(2)}, u32[]{:S(2)}) collective-permute-start(bf16[256,512]{1,0:T(8,128)(2,1)S(1)} %constant_dynamic-slice_fusion), channel_id=1, source_target_pairs={{0,4},{1,5},{2,6},{3,7},{4,0},{5,1},{6,2},{7,3},{8,12},{9,13},{10,... | collective-permute-start | bytes 786440 | tf_op jit(solution)/shard_map/ppermute | solution.py:273
  19.3 0.0 collective-permute-done.9
  19.3 1.3 collective-permute-start.10
  20.6 18.1 %collective-permute-done.4.refs_2_ = bf16[256,512]{1,0:T(8,128)(2,1)} collective-permute-done((bf16[256,512]{1,0:T(8,128)(2,1)S(1)}, bf16[256,512]{1,0:T(8,128)(2,1)}, u32[]{:S(2)}, u32[]{:S(2)}) %collective-permute-start.4) | collective-permute-done | bytes 262176 | tf_op jit(solution)/shard_map/ppermute | solution.py:273
  38.7 1.4 collective-permute-start.8
  40.1 1.0 collective-permute-start.3
  41.1 14.0 %collective-permute-done.10 = bf16[256,512]{1,0:T(8,128)(2,1)} collective-permute-done((bf16[256,512]{1,0:T(8,128)(2,1)}, bf16[256,512]{1,0:T(8,128)(2,1)}, u32[]{:S(2)}, u32[]{:S(2)}) %collective-permute-start.10) | collective-permute-done | bytes 262176 | tf_op jit(solution)/shard_map/ppermute | solution.py:273
  55.2 1.5 collective-permute-start.6
  56.6 0.0 collective-permute-done.8
  56.6 1.3 collective-permute-start.14
  57.9 1.7 %broadcast_select_fusion.1.refs_6_ = bf16[256,512]{1,0:T(8,128)(2,1)} fusion(bf16[256,512]{1,0:T(8,128)(2,1)} %collective-permute-done.8, bf16[256,512]{1,0:T(8,128)(2,1)} %collective-permute-done.10, pred[]{:T(512)S(6)} %or.3), kind=kLoop, calls=%fused_computation.1 | loop fusion | flops 131072 | bytes 786433 | tf_op jit(solution)/shard_map/jit(_where)/select_n | solution.py:250
  59.6 0.0 collective-permute-done.1.og_sib
  59.6 1.5 collective-permute-start.5
  61.1 0.0 collective-permute-done.tok_sib
  61.1 0.6 collective-permute-start.12
  61.7 0.0 all-to-all-done.blocks
  61.7 0.7 copy-done.1
  62.5 1.1 copy-done
  63.5 5.9 %shard_map.103 = (bf16[8,128,512]{2,1,0:T(8,128)(2,1)}, f32[256,64]{1,0:T(8,128)}, bf16[128,64]{1,0:T(8,128)(2,1)}, bf16[128,64]{1,0:T(8,128)(2,1)}, bf16[512,64]{1,0:T(8,128)(2,1)}) custom-call(s32[3]{0:T(128)} %pad_add_fusion.meta, s32[16]{0:T(128)} %bitcast.5, s32[16]{0:T(128)} %ranks.3, bf16[128,8192]{1,0:T(8,128)(2,1)} %tok_own.3, ...), custom_call_target="tpu_custom_call" | custom-call | flops 268435456 | bytes 6848512 | tf_op jit(solution)/shard_map/pallas_call | solution.py:25
  69.5 6.7 %all-to-all-start.1 = ((bf16[8,128,512]{2,1,0:T(8,128)(2,1)}), bf16[8,128,512]{2,1,0:T(8,128)(2,1)S(1)}, u32[]{:S(2)}, u32[]{:S(2)}) async-start(bf16[8,128,512]{2,1,0:T(8,128)(2,1)} %get-tuple-element.35), calls=%async_computation.1 | async-start | bytes 2097152 | tf_op jit(solution)/shard_map/all_to_all | solution.py:281
  76.2 1.0 broadcast_select_fusion.refs_10_
  77.2 2.1 %collective-permute-start.16 = (bf16[256,512]{1,0:T(8,128)(2,1)S(1)}, bf16[256,512]{1,0:T(8,128)(2,1)S(1)}, u32[]{:S(2)}, u32[]{:S(2)}) collective-permute-start(bf16[256,512]{1,0:T(8,128)(2,1)S(1)} %broadcast_select_fusion.refs_10_), channel_id=1, source_target_pairs={{0,2},{1,3},{2,0},{3,1},{4,6},{5,7},{6,4},{7,5},{8,10},{9,11},{10,... | collective-permute-start | bytes 786440 | tf_op jit(solution)/shard_map/ppermute | solution.py:273
  79.3 0.5 collective-permute-start.11
  79.8 1.5 collective-permute-start.7
  81.3 0.5 collective-permute-start.15
  81.9 1.5 collective-permute-start.13
  83.3 9.7 %collective-permute-done.16.refs_12_ = bf16[256,512]{1,0:T(8,128)(2,1)S(1)} collective-permute-done((bf16[256,512]{1,0:T(8,128)(2,1)S(1)}, bf16[256,512]{1,0:T(8,128)(2,1)S(1)}, u32[]{:S(2)}, u32[]{:S(2)}) %collective-permute-start.16) | collective-permute-done | bytes 262176 | tf_op jit(solution)/shard_map/ppermute | solution.py:273
  93.1 0.5 collective-permute-start.17
  93.6 0.8 collective-permute-done.7.refs_5_
  94.4 11.1 %collective-permute-done.13.refs_9_ = bf16[256,512]{1,0:T(8,128)(2,1)S(1)} collective-permute-done((bf16[256,512]{1,0:T(8,128)(2,1)}, bf16[256,512]{1,0:T(8,128)(2,1)S(1)}, u32[]{:S(2)}, u32[]{:S(2)}) %collective-permute-start.13) | collective-permute-done | bytes 262176 | tf_op jit(solution)/shard_map/ppermute | solution.py:273
  105.4 2.8 %collective-permute-done.17.refs_13_ = bf16[256,512]{1,0:T(8,128)(2,1)S(1)} collective-permute-done((bf16[256,512]{1,0:T(8,128)(2,1)S(1)}, bf16[256,512]{1,0:T(8,128)(2,1)S(1)}, u32[]{:S(2)}, u32[]{:S(2)}) %collective-permute-start.17) | collective-permute-done | bytes 262176 | tf_op jit(solution)/shard_map/ppermute | solution.py:273
  108.3 0.7 copy-done.13
  109.0 8.2 %shard_map.104 = (f32[128,512]{1,0:T(8,128)}, f32[128,512]{1,0:T(8,128)}, bf16[128,4096]{1,0:T(8,128)(2,1)}, bf16[128,4096]{1,0:T(8,128)(2,1)}) custom-call(s32[3]{0:T(128)} %pad_add_fusion.meta, bf16[128,8192]{1,0:T(8,128)(2,1)} %tok_own.3, bf16[128,8192]{1,0:T(8,128)(2,1)} %copy-done.1, bf16[128,512]{1,0:T(8,128)(2,1)} %og_own.5, ...), custom_call_target="tpu_custom_call" | custom-call | flops 2147483648 | bytes 12484608 | tf_op jit(solution)/shard_map/pallas_call | solution.py:25
  117.1 0.5 collective-permute-start.18
  117.6 0.1 collective-permute-start.19
  117.7 2.4 %collective-permute-done.19.other = f32[256,64]{1,0:T(8,128)S(1)} collective-permute-done((f32[256,64]{1,0:T(8,128)S(1)}, f32[256,64]{1,0:T(8,128)S(1)}, u32[]{:S(2)}, u32[]{:S(2)}) %collective-permute-start.19) | collective-permute-done | bytes 65568 | tf_op jit(solution)/shard_map/ppermute | solution.py:273
  120.2 0.7 copy-done.15
  120.8 2.8 %shard_map.105 = (f32[128,512]{1,0:T(8,128)}, bf16[8,512]{1,0:T(8,128)(2,1)}, bf16[8,512]{1,0:T(8,128)(2,1)}, bf16[8,512]{1,0:T(8,128)(2,1)}, bf16[8,512]{1,0:T(...) custom-call(s32[3]{0:T(128)} %pad_add_fusion.meta, ...), custom_call_target="tpu_custom_call" | custom-call | flops 16777216 | bytes 786432 | tf_op jit(solution)/shard_map/pallas_call | solution.py:25
  123.6 0.4 collective-permute-start.21
  124.0 1.6 %collective-permute-start.22 = (bf16[8,512]{1,0:T(8,128)(2,1)}, bf16[8,512]{1,0:T(8,128)(2,1)S(1)}, u32[]{:S(2)}, u32[]{:S(2)}) collective-permute-start(bf16[8,512]{1,0:T(8,128)(2,1)} %get-tuple-element.38), channel_id=1, source_target_pairs={{0,4},{1,5},{2,6},{3,7},{4,0},{5,1},{6,2},{7,3},{8,12},{9,13},{10,... | collective-permute-start | bytes 24584 | tf_op jit(solution)/shard_map/ppermute | solution.py:273
  125.7 1.5 collective-permute-start.23
  127.1 0.4 collective-permute-done.21.refs_1_
  127.5 2.4 %collective-permute-start.24 = (bf16[8,512]{1,0:T(8,128)(2,1)}, bf16[8,512]{1,0:T(8,128)(2,1)S(1)}, u32[]{:S(2)}, u32[]{:S(2)}) collective-permute-start(bf16[8,512]{1,0:T(8,128)(2,1)} %get-tuple-element.40), channel_id=1, source_target_pairs={{0,8},{1,9},{2,10},{3,11},{4,12},{5,13},{6,14},{7,15},{8,0},{9,1},... | collective-permute-start | bytes 24584 | tf_op jit(solution)/shard_map/ppermute | solution.py:273
  129.9 1.5 collective-permute-start.25
  131.3 2.4 %collective-permute-start.26 = (bf16[8,512]{1,0:T(8,128)(2,1)}, bf16[8,512]{1,0:T(8,128)(2,1)S(1)}, u32[]{:S(2)}, u32[]{:S(2)}) collective-permute-start(bf16[8,512]{1,0:T(8,128)(2,1)} %get-tuple-element.42), channel_id=1, source_target_pairs={{0,12},{1,13},{2,14},{3,15},{4,8},{5,9},{6,10},{7,11},{8,4},{9,5},... | collective-permute-start | bytes 24584 | tf_op jit(solution)/shard_map/ppermute | solution.py:273
  133.7 1.9 %collective-permute-start.27 = (bf16[8,512]{1,0:T(8,128)(2,1)}, bf16[8,512]{1,0:T(8,128)(2,1)S(1)}, u32[]{:S(2)}, u32[]{:S(2)}) collective-permute-start(bf16[8,512]{1,0:T(8,128)(2,1)} %get-tuple-element.43), channel_id=1, source_target_pairs={{0,14},{1,15},{2,12},{3,13},{4,10},{5,11},{6,8},{7,9},{8,6},{9,7},... | collective-permute-start | bytes 24584 | tf_op jit(solution)/shard_map/ppermute | solution.py:273
  135.6 1.4 collective-permute-done.26.refs_6_
  137.0 3.3 %collective-permute-done.27.refs_7_ = bf16[8,512]{1,0:T(8,128)(2,1)S(1)} collective-permute-done((bf16[8,512]{1,0:T(8,128)(2,1)}, bf16[8,512]{1,0:T(8,128)(2,1)S(1)}, u32[]{:S(2)}, u32[]{:S(2)}) %collective-permute-start.27) | collective-permute-done | bytes 8224 | tf_op jit(solution)/shard_map/ppermute | solution.py:273
  140.3 0.6 copy-done.23
  140.9 1.6 %shard_map.108 = bf16[16,2048]{1,0:T(8,128)(2,1)} custom-call(s32[3]{0:T(128)} %pad_add_fusion.meta, s32[16]{0:T(128)} %bitcast.7, bf16[8,512]{1,0:T(8,128)(2,1)} %get-tuple-element.36.refs_0_, bf16[8,512]{1,0:T(8,128)(2,1)} %copy-done.17, bf16[8,512]{1,0:T(8,128)(2,1)} %copy-done.18, bf16[8,512]{1,0:T(8,128)(2,1)} %copy-done.19, bf16[8,512]{1,0:T(8,128)(2,1)} %copy-done.20, ...), custom_call_target="tpu_custom_call" | custom-call | bytes 131072 | tf_op jit(solution)/shard_map/pallas_call | solution.py:25
  142.5 0.7 copy-done.7
  143.2 0.4 copy-done.5
  143.6 3.4 %shard_map.106 = (bf16[128,512]{1,0:T(8,128)(2,1)}, bf16[128,8192]{1,0:T(8,128)(2,1)}) custom-call(s32[3]{0:T(128)} %pad_add_fusion.meta, f32[128,512]{1,0:T(8,128)} %get-tuple-element.26.mine, f32[128,512]{1,0:T(8,128)} %copy-done.7, f32[128,512]{1,0:T(8,128)} %get-tuple-element.30.out_low, bf16[128,4096]{1,0:T(8,128)(2,1)} %get-tuple-element.31.grad_mine, ...), custom_call_target="tpu_custom_call" | custom-call | bytes 5111808 | tf_op jit(solution)/shard_map/pallas_call | solution.py:25
  147.0 1.0 copy-done.2
  148.0 2.3 %shard_map.107 = bf16[16,64,512]{2,1,0:T(8,128)(2,1)} custom-call(s32[3]{0:T(128)} %pad_add_fusion.meta, s32[16]{0:T(128)} %bitcast.8, bf16[8,128,512]{2,1,0:T(8,128)(2,1)} %copy-done.2), custom_call_target="tpu_custom_call" | custom-call | bytes 2097152 | tf_op jit(solution)/shard_map/pallas_call | solution.py:25
  (55 shorter events, 0.1 us)
Async XLA Ops:
  0.6 1.6 %collective-permute-start.2 = (bf16[16,2048]{1,0:T(8,128)(2,1)}, bf16[16,2048]{1,0:T(8,128)(2,1)S(1)}, u32[]{:S(2)}, u32[]{:S(2)}) collective-permute-start(bf16[16,2048]{1,0:T(8,128)(2,1)} %up_own.1), channel_id=1, source_target_pairs={{0,1},{1,0},{2,3},{3,2},{4,5},{5,4},{6,7},{7,6},{8,9},{9,8},{10,11... | collective-permute-start | bytes 196616 | tf_op jit(solution)/shard_map/ppermute | solution.py:273
  1.1 60.0 %collective-permute-start = (bf16[128,8192]{1,0:T(8,128)(2,1)}, bf16[128,8192]{1,0:T(8,128)(2,1)S(1)}, u32[]{:S(2)}, u32[]{:S(2)}) collective-permute-start(bf16[128,8192]{1,0:T(8,128)(2,1)} %tok_own.3), channel_id=1, source_target_pairs={{0,1},{1,0},{2,3},{3,2},{4,5},{5,4},{6,7},{7,6},{8,9},{9,8},{10,11... | collective-permute-start | bytes 6291464 | tf_op jit(solution)/shard_map/ppermute | solution.py:273
  2.3 0.6 copy-start.16
  2.9 38.2 %copy-start.3 = (bf16[128,512]{1,0:T(8,128)(2,1)S(1)}, bf16[128,512]{1,0:T(8,128)(2,1)}, u32[]{:S(2)}) copy-start(bf16[128,512]{1,0:T(8,128)(2,1)} %og_own.5) | copy-start | bytes 393220
  5.7 56.0 %all-to-all-start = ((bf16[8,144,512]{2,1,0:T(8,128)(2,1)}), bf16[8,144,512]{2,1,0:T(8,128)(2,1)S(1)}, u32[]{:S(2)}, u32[]{:S(2)}) async-start(bf16[8,144,512]{2,1,0:T(8,128)(2,1)} %shard_map.102), calls=%async_computation | async-start | bytes 2359296 | tf_op jit(solution)/shard_map/all_to_all | solution.py:281
  13.9 5.5 %collective-permute-start.9 = (bf16[256,512]{1,0:T(8,128)(2,1)S(1)}, bf16[256,512]{1,0:T(8,128)(2,1)}, u32[]{:S(2)}, u32[]{:S(2)}) collective-permute-start(bf16[256,512]{1,0:T(8,128)(2,1)S(1)} %constant_dynamic-slice_fusion), channel_id=1, source_target_pairs={{4,8},{5,9},{6,10},{7,11},{8,4},{9,5},{10,6},{11,7},{20,24},{21,25... | collective-permute-start | bytes 786440 | tf_op jit(solution)/shard_map/ppermute | solution.py:273
  15.2 23.5 %collective-permute-start.4 = (bf16[256,512]{1,0:T(8,128)(2,1)S(1)}, bf16[256,512]{1,0:T(8,128)(2,1)}, u32[]{:S(2)}, u32[]{:S(2)}) collective-permute-start(bf16[256,512]{1,0:T(8,128)(2,1)S(1)} %constant_dynamic-slice_fusion), channel_id=1, source_target_pairs={{0,4},{1,5},{2,6},{3,7},{4,0},{5,1},{6,2},{7,3},{8,12},{9,13},{10,... | collective-permute-start | bytes 786440 | tf_op jit(solution)/shard_map/ppermute | solution.py:273
  19.3 35.8 %collective-permute-start.10 = (bf16[256,512]{1,0:T(8,128)(2,1)}, bf16[256,512]{1,0:T(8,128)(2,1)}, u32[]{:S(2)}, u32[]{:S(2)}) collective-permute-start(bf16[256,512]{1,0:T(8,128)(2,1)} %collective-permute-done.9), channel_id=1, source_target_pairs={{4,0},{5,1},{6,2},{7,3},{8,12},{9,13},{10,14},{11,15},{20,16},{21,... | collective-permute-start | bytes 786440 | tf_op jit(solution)/shard_map/ppermute | solution.py:273
  38.7 17.9 %collective-permute-start.8 = (bf16[256,512]{1,0:T(8,128)(2,1)}, bf16[256,512]{1,0:T(8,128)(2,1)}, u32[]{:S(2)}, u32[]{:S(2)}) collective-permute-start(bf16[256,512]{1,0:T(8,128)(2,1)} %collective-permute-done.4.refs_2_), channel_id=1, source_target_pairs={{4,8},{5,9},{6,10},{7,11},{8,4},{9,5},{10,6},{11,7},{20,24},{21,25... | collective-permute-start | bytes 786440 | tf_op jit(solution)/shard_map/ppermute | solution.py:273
  40.1 41.2 %collective-permute-start.3 = (bf16[512,512]{1,0:T(8,128)(2,1)}, bf16[512,512]{1,0:T(8,128)(2,1)}, u32[]{:S(2)}, u32[]{:S(2)}) collective-permute-start(bf16[512,512]{1,0:T(8,128)(2,1)} %refs_0_.1), channel_id=1, source_target_pairs={{0,2},{1,3},{2,0},{3,1},{4,6},{5,7},{6,4},{7,5},{8,10},{9,11},{10,... | collective-permute-start | bytes 1572872 | tf_op jit(solution)/shard_map/ppermute | solution.py:273
  41.1 18.5 %collective-permute-start.1 = (bf16[128,512]{1,0:T(8,128)(2,1)S(1)}, bf16[128,512]{1,0:T(8,128)(2,1)S(1)}, u32[]{:S(2)}, u32[]{:S(2)}) collective-permute-start(bf16[128,512]{1,0:T(8,128)(2,1)S(1)} %copy-done.3), channel_id=1, source_target_pairs={{0,1},{1,0},{2,3},{3,2},{4,5},{5,4},{6,7},{7,6},{8,9},{9,8},{10,11... | collective-permute-start | bytes 393224 | tf_op jit(solution)/shard_map/ppermute | solution.py:273
  55.2 24.1 %collective-permute-start.6 = (bf16[256,512]{1,0:T(8,128)(2,1)}, bf16[256,512]{1,0:T(8,128)(2,1)}, u32[]{:S(2)}, u32[]{:S(2)}) collective-permute-start(bf16[256,512]{1,0:T(8,128)(2,1)} %collective-permute-done.4.refs_2_), channel_id=1, source_target_pairs={{0,2},{1,3},{2,0},{3,1},{4,6},{5,7},{6,4},{7,5},{8,10},{9,11},{10,... | collective-permute-start | bytes 786440 | tf_op jit(solution)/shard_map/ppermute | solution.py:273
  56.6 19.5 %collective-permute-start.14 = (bf16[256,512]{1,0:T(8,128)(2,1)}, bf16[256,512]{1,0:T(8,128)(2,1)}, u32[]{:S(2)}, u32[]{:S(2)}) collective-permute-start(bf16[256,512]{1,0:T(8,128)(2,1)} %collective-permute-done.8), channel_id=1, source_target_pairs={{4,0},{5,1},{6,2},{7,3},{8,12},{9,13},{10,14},{11,15},{20,16},{21,... | collective-permute-start | bytes 786440 | tf_op jit(solution)/shard_map/ppermute | solution.py:273
  59.6 2.1 %copy-start.4 = (bf16[128,512]{1,0:T(8,128)(2,1)}, bf16[128,512]{1,0:T(8,128)(2,1)S(1)}, u32[]{:S(2)}) copy-start(bf16[128,512]{1,0:T(8,128)(2,1)S(1)} %collective-permute-done.1.og_sib) | copy-start | bytes 393220
  59.6 20.2 %collective-permute-start.5 = (bf16[256,512]{1,0:T(8,128)(2,1)}, bf16[256,512]{1,0:T(8,128)(2,1)}, u32[]{:S(2)}, u32[]{:S(2)}) collective-permute-start(bf16[256,512]{1,0:T(8,128)(2,1)} %collective-permute-done.4.refs_2_), channel_id=1, source_target_pairs={{0,16},{1,17},{2,18},{3,19},{4,20},{5,21},{6,22},{7,23},{8,24},{9,... | collective-permute-start | bytes 786440 | tf_op jit(solution)/shard_map/ppermute | solution.py:273
  61.1 1.3 copy-start.1
  61.1 20.7 %collective-permute-start.12 = (bf16[256,512]{1,0:T(8,128)(2,1)}, bf16[256,512]{1,0:T(8,128)(2,1)}, u32[]{:S(2)}, u32[]{:S(2)}) collective-permute-start(bf16[256,512]{1,0:T(8,128)(2,1)} %broadcast_select_fusion.1.refs_6_), channel_id=1, source_target_pairs={{0,2},{1,3},{2,0},{3,1},{4,6},{5,7},{6,4},{7,5},{8,10},{9,11},{10,... | collective-permute-start | bytes 786440 | tf_op jit(solution)/shard_map/ppermute | solution.py:273
  62.5 1.1 copy-start
  69.5 77.5 %all-to-all-start.1 = ((bf16[8,128,512]{2,1,0:T(8,128)(2,1)}), bf16[8,128,512]{2,1,0:T(8,128)(2,1)S(1)}, u32[]{:S(2)}, u32[]{:S(2)}) async-start(bf16[8,128,512]{2,1,0:T(8,128)(2,1)} %get-tuple-element.35), calls=%async_computation.1 | async-start | bytes 2097152 | tf_op jit(solution)/shard_map/all_to_all | solution.py:281
  77.2 31.0 %copy-start.6 = (bf16[256,512]{1,0:T(8,128)(2,1)}, bf16[256,512]{1,0:T(8,128)(2,1)S(1)}, u32[]{:S(2)}) copy-start(bf16[256,512]{1,0:T(8,128)(2,1)S(1)} %broadcast_select_fusion.refs_10_) | copy-start | bytes 786436
  77.2 15.8 %collective-permute-start.16 = (bf16[256,512]{1,0:T(8,128)(2,1)S(1)}, bf16[256,512]{1,0:T(8,128)(2,1)S(1)}, u32[]{:S(2)}, u32[]{:S(2)}) collective-permute-start(bf16[256,512]{1,0:T(8,128)(2,1)S(1)} %broadcast_select_fusion.refs_10_), channel_id=1, source_target_pairs={{0,2},{1,3},{2,0},{3,1},{4,6},{5,7},{6,4},{7,5},{8,10},{9,11},{10,... | collective-permute-start | bytes 786440 | tf_op jit(solution)/shard_map/ppermute | solution.py:273
  79.3 14.3 %collective-permute-start.11 = (bf16[256,512]{1,0:T(8,128)(2,1)}, bf16[256,512]{1,0:T(8,128)(2,1)S(1)}, u32[]{:S(2)}, u32[]{:S(2)}) collective-permute-start(bf16[256,512]{1,0:T(8,128)(2,1)} %broadcast_select_fusion.1.refs_6_), channel_id=1, source_target_pairs={{0,16},{1,17},{2,18},{3,19},{4,20},{5,21},{6,22},{7,23},{8,24},{9,... | collective-permute-start | bytes 786440 | tf_op jit(solution)/shard_map/ppermute | solution.py:273
  79.8 14.5 %collective-permute-start.7 = (bf16[256,512]{1,0:T(8,128)(2,1)}, bf16[256,512]{1,0:T(8,128)(2,1)S(1)}, u32[]{:S(2)}, u32[]{:S(2)}) collective-permute-start(bf16[256,512]{1,0:T(8,128)(2,1)} %collective-permute-done.6.refs_4_), channel_id=1, source_target_pairs={{0,16},{1,17},{2,18},{3,19},{4,20},{5,21},{6,22},{7,23},{8,24},{9,... | collective-permute-start | bytes 786440 | tf_op jit(solution)/shard_map/ppermute | solution.py:273
  81.3 24.1 %collective-permute-start.15 = (bf16[256,512]{1,0:T(8,128)(2,1)S(1)}, bf16[256,512]{1,0:T(8,128)(2,1)S(1)}, u32[]{:S(2)}, u32[]{:S(2)}) collective-permute-start(bf16[256,512]{1,0:T(8,128)(2,1)S(1)} %broadcast_select_fusion.refs_10_), channel_id=1, source_target_pairs={{0,16},{1,17},{2,18},{3,19},{4,20},{5,21},{6,22},{7,23},{8,24},{9,... | collective-permute-start | bytes 786440 | tf_op jit(solution)/shard_map/ppermute | solution.py:273
  81.9 23.6 %collective-permute-start.13 = (bf16[256,512]{1,0:T(8,128)(2,1)}, bf16[256,512]{1,0:T(8,128)(2,1)S(1)}, u32[]{:S(2)}, u32[]{:S(2)}) collective-permute-start(bf16[256,512]{1,0:T(8,128)(2,1)} %collective-permute-done.12.refs_8_), channel_id=1, source_target_pairs={{0,16},{1,17},{2,18},{3,19},{4,20},{5,21},{6,22},{7,23},{8,24},{9,... | collective-permute-start | bytes 786440 | tf_op jit(solution)/shard_map/ppermute | solution.py:273
  93.0 15.2 %copy-start.8 = (bf16[256,512]{1,0:T(8,128)(2,1)}, bf16[256,512]{1,0:T(8,128)(2,1)S(1)}, u32[]{:S(2)}) copy-start(bf16[256,512]{1,0:T(8,128)(2,1)S(1)} %collective-permute-done.16.refs_12_) | copy-start | bytes 786436
  93.1 15.2 %collective-permute-start.17 = (bf16[256,512]{1,0:T(8,128)(2,1)S(1)}, bf16[256,512]{1,0:T(8,128)(2,1)S(1)}, u32[]{:S(2)}, u32[]{:S(2)}) collective-permute-start(bf16[256,512]{1,0:T(8,128)(2,1)S(1)} %collective-permute-done.16.refs_12_), channel_id=1, source_target_pairs={{0,16},{1,17},{2,18},{3,19},{4,20},{5,21},{6,22},{7,23},{8,24},{9,... | collective-permute-start | bytes 786440 | tf_op jit(solution)/shard_map/ppermute | solution.py:273
  93.6 14.7 %copy-start.9 = (bf16[256,512]{1,0:T(8,128)(2,1)}, bf16[256,512]{1,0:T(8,128)(2,1)S(1)}, u32[]{:S(2)}) copy-start(bf16[256,512]{1,0:T(8,128)(2,1)S(1)} %collective-permute-done.11.refs_7_) | copy-start | bytes 786436
  94.4 13.9 %copy-start.10 = (bf16[256,512]{1,0:T(8,128)(2,1)}, bf16[256,512]{1,0:T(8,128)(2,1)S(1)}, u32[]{:S(2)}) copy-start(bf16[256,512]{1,0:T(8,128)(2,1)S(1)} %collective-permute-done.7.refs_5_) | copy-start | bytes 786436
  105.4 2.8 %copy-start.12 = (bf16[256,512]{1,0:T(8,128)(2,1)}, bf16[256,512]{1,0:T(8,128)(2,1)S(1)}, u32[]{:S(2)}) copy-start(bf16[256,512]{1,0:T(8,128)(2,1)S(1)} %collective-permute-done.13.refs_9_) | copy-start | bytes 786436
  105.4 2.8 %copy-start.11 = (bf16[256,512]{1,0:T(8,128)(2,1)}, bf16[256,512]{1,0:T(8,128)(2,1)S(1)}, u32[]{:S(2)}) copy-start(bf16[256,512]{1,0:T(8,128)(2,1)S(1)} %collective-permute-done.15.refs_11_) | copy-start | bytes 786436
  108.2 0.7 copy-start.13
  109.0 8.7 %copy-start.14 = (f32[256,64]{1,0:T(8,128)S(1)}, f32[256,64]{1,0:T(8,128)}, u32[]{:S(2)}) copy-start(f32[256,64]{1,0:T(8,128)} %get-tuple-element.28.low) | copy-start | bytes 196612
  117.1 25.4 %collective-permute-start.20 = (bf16[128,4096]{1,0:T(8,128)(2,1)}, bf16[128,4096]{1,0:T(8,128)(2,1)S(1)}, u32[]{:S(2)}, u32[]{:S(2)}) collective-permute-start(bf16[128,4096]{1,0:T(8,128)(2,1)} %get-tuple-element.32), channel_id=1, source_target_pairs={{0,1},{1,0},{2,3},{3,2},{4,5},{5,4},{6,7},{7,6},{8,9},{9,8},{10,11... | collective-permute-start | bytes 3145736 | tf_op jit(solution)/shard_map/ppermute | solution.py:273
  117.1 25.4 %collective-permute-start.18 = (f32[128,512]{1,0:T(8,128)}, f32[128,512]{1,0:T(8,128)S(1)}, u32[]{:S(2)}, u32[]{:S(2)}) collective-permute-start(f32[128,512]{1,0:T(8,128)} %get-tuple-element.27), channel_id=1, source_target_pairs={{0,1},{1,0},{2,3},{3,2},{4,5},{5,4},{6,7},{7,6},{8,9},{9,8},{10,11... | collective-permute-start | bytes 786440 | tf_op jit(solution)/shard_map/ppermute | solution.py:273
  117.6 2.5 %collective-permute-start.19 = (f32[256,64]{1,0:T(8,128)S(1)}, f32[256,64]{1,0:T(8,128)S(1)}, u32[]{:S(2)}, u32[]{:S(2)}) collective-permute-start(f32[256,64]{1,0:T(8,128)S(1)} %copy-done.14), channel_id=1, source_target_pairs={{0,1},{1,0},{2,3},{3,2},{4,5},{5,4},{6,7},{7,6},{8,9},{9,8},{10,11... | collective-permute-start | bytes 196616 | tf_op jit(solution)/shard_map/ppermute | solution.py:273
  120.2 0.7 copy-start.15
  123.6 3.9 %collective-permute-start.21 = (bf16[8,512]{1,0:T(8,128)(2,1)}, bf16[8,512]{1,0:T(8,128)(2,1)S(1)}, u32[]{:S(2)}, u32[]{:S(2)}) collective-permute-start(bf16[8,512]{1,0:T(8,128)(2,1)} %get-tuple-element.37), channel_id=1, source_target_pairs={{0,2},{1,3},{2,0},{3,1},{4,6},{5,7},{6,4},{7,5},{8,10},{9,11},{10,... | collective-permute-start | bytes 24584 | tf_op jit(solution)/shard_map/ppermute | solution.py:273
  124.0 5.9 %collective-permute-start.22 = (bf16[8,512]{1,0:T(8,128)(2,1)}, bf16[8,512]{1,0:T(8,128)(2,1)S(1)}, u32[]{:S(2)}, u32[]{:S(2)}) collective-permute-start(bf16[8,512]{1,0:T(8,128)(2,1)} %get-tuple-element.38), channel_id=1, source_target_pairs={{0,4},{1,5},{2,6},{3,7},{4,0},{5,1},{6,2},{7,3},{8,12},{9,13},{10,... | collective-permute-start | bytes 24584 | tf_op jit(solution)/shard_map/ppermute | solution.py:273
  125.7 5.7 %collective-permute-start.23 = (bf16[8,512]{1,0:T(8,128)(2,1)}, bf16[8,512]{1,0:T(8,128)(2,1)S(1)}, u32[]{:S(2)}, u32[]{:S(2)}) collective-permute-start(bf16[8,512]{1,0:T(8,128)(2,1)} %get-tuple-element.39), channel_id=1, source_target_pairs={{0,6},{1,7},{2,4},{3,5},{4,2},{5,3},{6,0},{7,1},{8,14},{9,15},{10,... | collective-permute-start | bytes 24584 | tf_op jit(solution)/shard_map/ppermute | solution.py:273
  127.5 12.8 %copy-start.17 = (bf16[8,512]{1,0:T(8,128)(2,1)}, bf16[8,512]{1,0:T(8,128)(2,1)S(1)}, u32[]{:S(2)}) copy-start(bf16[8,512]{1,0:T(8,128)(2,1)S(1)} %collective-permute-done.21.refs_1_) | copy-start | bytes 24580
  127.5 6.2 %collective-permute-start.24 = (bf16[8,512]{1,0:T(8,128)(2,1)}, bf16[8,512]{1,0:T(8,128)(2,1)S(1)}, u32[]{:S(2)}, u32[]{:S(2)}) collective-permute-start(bf16[8,512]{1,0:T(8,128)(2,1)} %get-tuple-element.40), channel_id=1, source_target_pairs={{0,8},{1,9},{2,10},{3,11},{4,12},{5,13},{6,14},{7,15},{8,0},{9,1},... | collective-permute-start | bytes 24584 | tf_op jit(solution)/shard_map/ppermute | solution.py:273
  129.9 10.4 %copy-start.18 = (bf16[8,512]{1,0:T(8,128)(2,1)}, bf16[8,512]{1,0:T(8,128)(2,1)S(1)}, u32[]{:S(2)}) copy-start(bf16[8,512]{1,0:T(8,128)(2,1)S(1)} %collective-permute-done.22.refs_2_) | copy-start | bytes 24580
  129.9 5.8 %collective-permute-start.25 = (bf16[8,512]{1,0:T(8,128)(2,1)}, bf16[8,512]{1,0:T(8,128)(2,1)S(1)}, u32[]{:S(2)}, u32[]{:S(2)}) collective-permute-start(bf16[8,512]{1,0:T(8,128)(2,1)} %get-tuple-element.41), channel_id=1, source_target_pairs={{0,10},{1,11},{2,8},{3,9},{4,14},{5,15},{6,12},{7,13},{8,2},{9,3},... | collective-permute-start | bytes 24584 | tf_op jit(solution)/shard_map/ppermute | solution.py:273
  131.3 9.0 %copy-start.19 = (bf16[8,512]{1,0:T(8,128)(2,1)}, bf16[8,512]{1,0:T(8,128)(2,1)S(1)}, u32[]{:S(2)}) copy-start(bf16[8,512]{1,0:T(8,128)(2,1)S(1)} %collective-permute-done.23.refs_3_) | copy-start | bytes 24580
  131.3 5.7 %collective-permute-start.26 = (bf16[8,512]{1,0:T(8,128)(2,1)}, bf16[8,512]{1,0:T(8,128)(2,1)S(1)}, u32[]{:S(2)}, u32[]{:S(2)}) collective-permute-start(bf16[8,512]{1,0:T(8,128)(2,1)} %get-tuple-element.42), channel_id=1, source_target_pairs={{0,12},{1,13},{2,14},{3,15},{4,8},{5,9},{6,10},{7,11},{8,4},{9,5},... | collective-permute-start | bytes 24584 | tf_op jit(solution)/shard_map/ppermute | solution.py:273
  133.7 6.6 %copy-start.20 = (bf16[8,512]{1,0:T(8,128)(2,1)}, bf16[8,512]{1,0:T(8,128)(2,1)S(1)}, u32[]{:S(2)}) copy-start(bf16[8,512]{1,0:T(8,128)(2,1)S(1)} %collective-permute-done.24.refs_4_) | copy-start | bytes 24580
  133.7 6.6 %collective-permute-start.27 = (bf16[8,512]{1,0:T(8,128)(2,1)}, bf16[8,512]{1,0:T(8,128)(2,1)S(1)}, u32[]{:S(2)}, u32[]{:S(2)}) collective-permute-start(bf16[8,512]{1,0:T(8,128)(2,1)} %get-tuple-element.43), channel_id=1, source_target_pairs={{0,14},{1,15},{2,12},{3,13},{4,10},{5,11},{6,8},{7,9},{8,6},{9,7},... | collective-permute-start | bytes 24584 | tf_op jit(solution)/shard_map/ppermute | solution.py:273
  135.6 4.7 %copy-start.21 = (bf16[8,512]{1,0:T(8,128)(2,1)}, bf16[8,512]{1,0:T(8,128)(2,1)S(1)}, u32[]{:S(2)}) copy-start(bf16[8,512]{1,0:T(8,128)(2,1)S(1)} %collective-permute-done.25.refs_5_) | copy-start | bytes 24580
  137.0 3.3 %copy-start.22 = (bf16[8,512]{1,0:T(8,128)(2,1)}, bf16[8,512]{1,0:T(8,128)(2,1)S(1)}, u32[]{:S(2)}) copy-start(bf16[8,512]{1,0:T(8,128)(2,1)S(1)} %collective-permute-done.26.refs_6_) | copy-start | bytes 24580
  140.3 0.6 copy-start.23
  142.5 0.7 copy-start.7
  142.5 1.1 copy-start.5
  147.0 1.0 copy-start.2
